TPU v7x, 32 devices: a whole 2x2x4 slice. The times are simulated.
32 devices in a mesh: ctx: 16 (over z, y, core), exp: 2 (over x).
Axes of the slice: x: 2, y: 2, z: 4, core: 2. Of those that a mesh axis runs over, the one named last changes fastest.
Arguments:
- ssm_input: bfloat16 [2048, 4096], P('ctx', 'exp'), may hold values from -6 to 6
- gate_input: bfloat16 [2048, 4096], P('ctx', 'exp'), may hold values from -6 to 6
- b_input: bfloat16 [2048, 1024], P('ctx', 'exp'), may hold values from -6 to 6
- c_input: bfloat16 [2048, 1024], P('ctx', 'exp'), may hold values from -6 to 6
- step_size: float32 [64, 2048], P('exp', 'ctx'), may hold values from 0.5 to 4096
- decay_rate: float32 [64], P('exp'), may hold values from 9.765625e-05 to 0.1
- norm_gain: float32 [4096], P('exp'), may hold values from 0.1 to 1.9
- out_weight: bfloat16 [4096, 2048], P('exp'), may hold values from -0.125 to 0.125
- stream: bfloat16 [2048, 2048], P('ctx', 'exp'), may hold values from -7 to 7
- moe_gain: float32 [2048], replicated, may hold values from 0.1 to 1.9
- router: bfloat16 [2048, 16], replicated, may hold values from -0.125 to 0.125
- expert_ids: int32 [2048, 6], P('ctx'), may hold values from 0 to 15, all different within a row; in each aligned block of 128 rows (0 to 127, 128 to 255, ...) at most 60 rows name the same one
- w_gate: bfloat16 [16, 1408, 2048], P('ctx', 'exp'), may hold values from -0.125 to 0.125
- w_up: bfloat16 [16, 1408, 2048], P('ctx', 'exp'), may hold values from -0.125 to 0.125
- w_down: bfloat16 [16, 1408, 2048], P('ctx', 'exp'), may hold values from -0.21875 to 0.21875
Outputs:
- layer_out: bfloat16 [2048, 2048], P('ctx', 'exp')
Inputs may be any that keep to these rules, and one draw needn't show every extreme that they name: `expert_ids`: each row names 6 different experts; among the 128 rows of one device (aligned blocks of 128 rows) no expert is named by more than 60 rows, a bound that some block reaches.
All inputs are finite; a program needn't handle non-finite values.
Results may differ from a plain program's by a relative error of at most 0.024.
Values may be sent and summed in bfloat16 or wider, within the bound.
No kernel may reach another device: no remote copies, remote signals or barrier semaphores. Data moves between devices by JAX's collectives and lax.ppermute only.
A program may use at most 128 MiB of HBM per device.

v0:
```python
import jax
import jax.numpy as jnp
from jax import lax
from jax.sharding import PartitionSpec as P

P_SIZE = 64
N = 128


def entering_2(part, axis, combine, identity):
    place = lax.axis_index(axis)
    gathered = jax.tree.map(lambda a: lax.all_gather(a, axis), part)
    state = jax.tree.map(lambda a, e: jnp.zeros_like(a) + jnp.asarray(e, a.dtype), part, identity)

    def one(step, state):
        return combine(
            state, jax.tree.map(lambda a: lax.dynamic_index_in_dim(a, step, 0, False), gathered)
        )

    return lax.fori_loop(0, place, one, state)


def chain_combine(earlier, later):
    return (earlier[0] * later[0], later[0][:, :, None, None] * earlier[1] + later[1])


def run_rows(pieces, w_gate, w_up, w_down):
    row_count = pieces.shape[0] * pieces.shape[1]
    flattened = pieces.reshape(row_count, pieces.shape[2])
    contract = (((1,), (1,)), ((), ()))
    gate_proj = lax.dot_general(flattened, w_gate[0], contract, preferred_element_type=jnp.float32)
    up_proj = lax.dot_general(flattened, w_up[0], contract, preferred_element_type=jnp.float32)
    active = (jax.nn.silu(gate_proj) * up_proj).astype(jnp.bfloat16)
    partial_value = jnp.dot(active, w_down[0], preferred_element_type=jnp.float32).astype(
        jnp.bfloat16
    )
    full_width = partial_value.shape[1]
    shaped = partial_value.reshape(pieces.shape[0], pieces.shape[1], full_width)
    return lax.all_to_all(shaped, "ctx", split_axis=0, concat_axis=0, tiled=True)


def per_device(
    ssm_input,
    gate_input,
    b_input,
    c_input,
    step_size,
    decay_rate,
    norm_gain,
    out_weight,
    stream,
    moe_gain,
    router,
    expert_ids,
    w_gate,
    w_up,
    w_down,
):
    token_count = ssm_input.shape[0]
    head_count = step_size.shape[0]
    group_count = b_input.shape[1] // N
    per_group = head_count // group_count
    log_decay = -step_size * decay_rate[:, None]
    running = jnp.cumsum(log_decay, axis=1).T.reshape(token_count, group_count, per_group)
    shaped_x = ssm_input.reshape(token_count, group_count, per_group, P_SIZE)
    step_rows = step_size.T.reshape(token_count, group_count, per_group)
    weighted = (step_rows[..., None] * shaped_x).astype(jnp.bfloat16)
    b_block = b_input.reshape(token_count, group_count, N)
    c_block = c_input.reshape(token_count, group_count, N)
    scores = jnp.einsum("tgn,sgn->gts", c_block, b_block, preferred_element_type=jnp.float32)
    ordered = running.transpose(1, 2, 0)
    spread = ordered[:, :, :, None] - ordered[:, :, None, :]
    lower_mask = jnp.arange(token_count)[:, None] >= jnp.arange(token_count)[None, :]
    decay_mat = jnp.where(lower_mask, jnp.exp(jnp.where(lower_mask, spread, 0.0)), 0.0)
    mixing = (decay_mat * scores[:, None]).astype(jnp.bfloat16)
    inner = jnp.einsum("gqts,sgqp->tgqp", mixing, weighted, preferred_element_type=jnp.float32)
    tail_decay = jnp.exp(running[-1:] - running)
    carried = (tail_decay[..., None] * weighted).astype(jnp.bfloat16)
    block_state = jnp.einsum("tgqp,tgn->gqpn", carried, b_block, preferred_element_type=jnp.float32)
    block_decay = jnp.exp(running[-1])
    identity = (jnp.ones_like(block_decay), jnp.zeros_like(block_state))
    entry_decay, entering = entering_2((block_decay, block_state), "ctx", chain_combine, identity)
    carried_in = jnp.einsum(
        "tgn,gqpn->tgqp", c_block.astype(jnp.float32), entering, precision=lax.Precision.HIGHEST
    )
    ssd_out = (inner + jnp.exp(running)[..., None] * carried_in).reshape(
        token_count, group_count, per_group * P_SIZE
    )
    gated = ssd_out * jax.nn.silu(gate_input.astype(jnp.float32)).reshape(
        token_count, group_count, per_group * P_SIZE
    )
    mean_sq = jnp.mean(gated * gated, axis=-1, keepdims=True)
    normed = (
        (gated * lax.rsqrt(mean_sq + 1e-05)).reshape(token_count, head_count * P_SIZE) * norm_gain
    ).astype(jnp.bfloat16)
    mixer = jnp.dot(normed, out_weight, preferred_element_type=jnp.float32)
    slice_width = stream.shape[1]
    start_col = lax.axis_index("exp") * slice_width
    expert_count = router.shape[1]
    top_count = expert_ids.shape[1]
    capacity = max(
        2, token_count * top_count // expert_count + token_count * top_count // (4 * expert_count)
    )
    own_cols = lax.dynamic_slice_in_dim(mixer, start_col, slice_width, 1) + stream.astype(
        jnp.float32
    )
    with_stream = lax.dynamic_update_slice_in_dim(mixer, own_cols, start_col, 1)
    hidden_all = lax.psum(with_stream.astype(jnp.bfloat16), "exp")
    hidden_own = lax.dynamic_slice_in_dim(hidden_all, start_col, slice_width, 1)
    hidden_f = hidden_all.astype(jnp.float32)
    mean_h = jnp.mean(hidden_f * hidden_f, axis=1, keepdims=True)
    sent_rows = (hidden_f * lax.rsqrt(mean_h + 1e-06) * moe_gain).astype(jnp.bfloat16)
    logits = jnp.dot(sent_rows, router, preferred_element_type=jnp.float32)
    sigmoid_score = jax.nn.sigmoid(logits)
    expert_range = jnp.arange(expert_count, dtype=jnp.int32)
    matches = expert_ids[:, :, None] == expert_range
    picked = jnp.sum(jnp.where(matches, sigmoid_score[:, None, :], 0.0), axis=2)
    gates = picked / jnp.sum(picked, axis=1, keepdims=True)
    flat_ids = expert_ids.reshape(-1)
    one_hot = (flat_ids[:, None] == expert_range).astype(jnp.int32)
    slot_index = jnp.sum((jnp.cumsum(one_hot, axis=0) - one_hot) * one_hot, axis=1)
    target = flat_ids * capacity + slot_index
    token_of = jnp.arange(token_count * top_count, dtype=jnp.int32) // top_count
    source_row = (
        jnp.full((expert_count * capacity,), token_count, jnp.int32).at[target].set(token_of)
    )
    padded = jnp.concatenate([sent_rows, jnp.zeros((1, sent_rows.shape[1]), jnp.bfloat16)], axis=0)
    outgoing = padded[source_row].reshape(expert_count, capacity, sent_rows.shape[1])
    returned = run_rows(
        lax.all_to_all(outgoing, "ctx", split_axis=0, concat_axis=0, tiled=True),
        w_gate,
        w_up,
        w_down,
    )
    back_width = returned.shape[2]
    flat_back = returned.reshape(expert_count * capacity, back_width)
    slot_rows = target.reshape(token_count, top_count)
    moe_part = jnp.zeros((token_count, back_width), jnp.float32)
    for choice_number in range(top_count):
        picked_rows = flat_back[slot_rows[:, choice_number]].astype(jnp.float32)
        moe_part = moe_part + gates[:, choice_number][:, None] * picked_rows
    moe_sum = lax.psum_scatter(
        moe_part.astype(jnp.bfloat16), "exp", scatter_dimension=1, tiled=True
    ).astype(jnp.float32)
    return (hidden_own.astype(jnp.float32) + moe_sum).astype(jnp.bfloat16)


def solution(mesh):
    in_specs = (
        P("ctx", "exp"),
        P("ctx", "exp"),
        P("ctx", "exp"),
        P("ctx", "exp"),
        P("exp", "ctx"),
        P("exp"),
        P("exp"),
        P("exp", None),
        P("ctx", "exp"),
        P(),
        P(),
        P("ctx", None),
        P("ctx", "exp", None),
        P("ctx", "exp", None),
        P("ctx", "exp", None),
    )
    out_specs = P("ctx", "exp")
    return jax.shard_map(
        per_device, mesh=mesh, in_specs=in_specs, out_specs=out_specs, check_vma=False
    )
```

profile of v0, /device:TPU:0, one launch (start us, length us, event | category | flops | bytes accessed | tf_op | source)
XLA Modules:
  0.0 528.1 jit_solution(1258037429971442725)
XLA Ops:
  34.8 24.0 %all_gather.10 = f32[16,4,8]{2,1,0:T(4,128)S(1)} all-gather(f32[1,4,8]{2,1,0:T(4,128)} %exp.44), channel_id=1, replica_groups=mesh['ctx'=16,'exp'=2] {'ctx'}, dimensions={0}, use_global_device_ids=true | all-gather | bytes 2176 | tf_op jit(solution)/shard_map/all_gather | solution.py:12
  62.0 81.7 %all-gather.3.cloned.1.call-done = f32[64,8,64,128]{3,2,1,0:T(8,128)} async-done(((f32[4,8,64,128]{3,2,1,0:T(8,128)}), f32[64,8,64,128]{3,2,1,0:T(8,128)}) %all-gather.3.cloned.1.call-update) | async-done | bytes 16777232 | tf_op jit(solution)/shard_map/all_gather | solution.py:12
  145.8 3.6 multiply_reduce_fusion
  155.1 5.5 %fusion.27 = f32[128,2048]{1,0:T(8,128)S(1)} fusion(bf16[2048,2048]{1,0:T(8,128)(2,1)} %param.24, f32[128,2048]{1,0:T(8,128)} %bitcast.108, f32[128,2048]{1,0:T(8,128)} %copy.66, f32[2048]{0:T(1024)S(1)} %copy-done.14, bf16[128,2048]{1,0:T(8,128)(2,1)S(1)} %copy-done.5), kind=kOutput, calls=%fused_computation.48 | convolution fusion | flops 1076101120 | bytes 12066816 | tf_op jit(solution)/shard_map/dot_general | solution.py:96
  161.7 3.4 scatter_custom_fusion
  165.1 63.5 %all-reduce.3.cloned.1.call-done = bf16[128,2048]{1,0:T(8,128)(2,1)} async-done(((bf16[128,2048]{1,0:T(8,128)(2,1)}), bf16[128,2048]{1,0:T(8,128)(2,1)}) %all-reduce.3.cloned.1.call-update) | async-done | bytes 524304 | tf_op jit(solution)/shard_map/psum | solution.py:108
  232.0 5.9 %gather_fusion = bf16[960,2048]{1,0:T(8,128)(2,1)} fusion(bf16[129,2048]{1,0:T(8,128)(2,1)S(1)} %concatenate.3, s32[1024]{0:T(1024)S(1)} %pad_clamp_fusion.6), kind=kCustom, calls=%fused_computation | custom fusion | bytes 7868160 | tf_op jit(solution)/shard_map/gather | solution.py:128
  237.9 4.9 reshape.141
  242.8 98.0 %all_to_all.10 = bf16[16,60,2048]{2,1,0:T(8,128)(2,1)} all-to-all(bf16[16,60,2048]{2,1,0:T(8,128)(2,1)} %reshape.141), channel_id=1, replica_groups=mesh['ctx'=16,'exp'=2] {'ctx'}, dimensions={0} | all-to-all | bytes 7864320 | tf_op jit(solution)/shard_map/all_to_all | solution.py:130
  340.8 4.8 reshape.142
  345.6 7.8 %fusion.1 = f32[960,704]{0,1:T(8,128)} fusion(bf16[960,2048]{1,0:T(8,128)(2,1)} %reshape.142, bf16[1,704,2048]{2,1,0:T(8,128)(2,1)} %param.30), kind=kOutput, calls=%fused_computation.12 | convolution fusion | flops 2768240640 | bytes 9519104 | tf_op jit(solution)/shard_map/dot_general | solution.py:32
  353.4 12.2 %convolution_convert_fusion = bf16[960,2048]{1,0:T(8,128)(2,1)} fusion(bf16[1,704,2048]{2,1,0:T(8,128)(2,1)S(1)} %copy-done, f32[960,704]{0,1:T(8,128)} %fusion.1, bf16[960,2048]{1,0:T(8,128)(2,1)} %reshape.142, bf16[1,704,2048]{2,1,0:T(8,128)(2,1)} %param.29), kind=kOutput, calls=%fused_computation.10 | convolution fusion | flops 5542502400 | bytes 16334848 | tf_op jit(solution)/shard_map/dot_general | solution.py:34
  365.6 4.9 reshape.143
  370.5 5.5 %all-to-all-start.1 = ((bf16[16,60,2048]{2,1,0:T(8,128)(2,1)}), bf16[16,60,2048]{2,1,0:T(8,128)(2,1)}, u32[]{:S(2)}, u32[]{:S(2)}) async-start(bf16[16,60,2048]{2,1,0:T(8,128)(2,1)} %reshape.143), calls=%async_computation.1 | async-start | bytes 8388608 | tf_op jit(solution)/shard_map/all_to_all | solution.py:39
  377.8 75.9 %all-to-all-done.1 = bf16[16,60,2048]{2,1,0:T(8,128)(2,1)} async-done(((bf16[16,60,2048]{2,1,0:T(8,128)(2,1)}), bf16[16,60,2048]{2,1,0:T(8,128)(2,1)}, u32[]{:S(2)}, u32[]{:S(2)}) %all-to-all-start.1) | async-done | bytes 3932192 | tf_op jit(solution)/shard_map/all_to_all | solution.py:39
  453.6 4.8 reshape.144
  458.5 4.9 gather_fusion.1
  463.3 4.9 gather_fusion.2
  468.2 4.9 gather_fusion.3
  473.1 4.9 gather_fusion.4
  478.0 4.8 gather_fusion.5
  482.8 4.9 gather_fusion.6
  487.7 3.4 add_convert_fusion
  491.1 28.7 %reduce-scatter.2.cloned.1.call-done = bf16[128,1024]{1,0:T(8,128)(2,1)} async-done(((bf16[128,2048]{1,0:T(8,128)(2,1)}), bf16[128,1024]{1,0:T(8,128)(2,1)}) %reduce-scatter.2.cloned.1.call-update) | async-done | bytes 262160 | tf_op jit(solution)/shard_map/reduce_scatter | solution.py:142
  (88 shorter events, 47.0 us)
Async XLA Ops:
  6.5 346.9 %copy-start = (bf16[1,704,2048]{2,1,0:T(8,128)(2,1)S(1)}, bf16[1,704,2048]{2,1,0:T(8,128)(2,1)}, u32[]{:S(2)}) copy-start(bf16[1,704,2048]{2,1,0:T(8,128)(2,1)} %param.31) | copy-start | bytes 8650756
  6.5 137.2 %all-gather.3.cloned.1.call-start = ((), (), s32[]{:S(2)}) async-start(), calls=%async_computation.5 | async-start | bytes 17825792 | tf_op jit(solution)/shard_map/all_gather | solution.py:12
  13.6 46.5 %copy-start.9 = (f32[32,128]{1,0:T(8,128)S(1)}, f32[32,128]{1,0:T(8,128)}, u32[]{:S(2)}) copy-start(f32[32,128]{1,0:T(8,128)} %param.21) | copy-start | bytes 49156
  13.6 215.0 %all-reduce.3.cloned.1.call-start = ((), (), s32[]{:S(2)}) async-start(), calls=%async_computation.3 | async-start | bytes 1048576 | tf_op jit(solution)/shard_map/psum | solution.py:108
  14.4 15.9 %copy-start.4 = (s32[128,6]{1,0:T(8,128)}, s32[128,6]{1,0:T(8,128)S(1)}, u32[]{:S(2)}) copy-start(s32[128,6]{1,0:T(8,128)S(1)} %copy.69) | copy-start | bytes 9220
  144.9 0.9 copy-start.6
  144.9 0.9 copy-start.8
  149.4 5.7 %copy-start.5 = (bf16[128,2048]{1,0:T(8,128)(2,1)S(1)}, bf16[128,2048]{1,0:T(8,128)(2,1)}, u32[]{:S(2)}) copy-start(bf16[128,2048]{1,0:T(8,128)(2,1)} %param.18) | copy-start | bytes 1572868
  149.4 5.7 %copy-start.14 = (f32[2048]{0:T(1024)S(1)}, f32[2048]{0:T(1024)}, u32[]{:S(2)}) copy-start(f32[2048]{0:T(1024)} %param.23) | copy-start | bytes 24580
  155.1 5.5 %copy-start.7 = (bf16[128,1024]{1,0:T(8,128)(2,1)S(1)}, bf16[128,1024]{1,0:T(8,128)(2,1)}, u32[]{:S(2)}) copy-start(bf16[128,1024]{1,0:T(8,128)(2,1)} %param.25) | copy-start | bytes 786436
  160.6 1.0 copy-start.10
  160.6 1.0 copy-start.12
  160.6 69.2 %copy-start.13 = (f32[2048]{0:T(1024)S(1)}, f32[2048]{0:T(1024)}, u32[]{:S(2)}) copy-start(f32[2048]{0:T(1024)} %param.26) | copy-start | bytes 24580
  231.1 0.8 copy-start.1
  370.5 6.1 %copy-start.2 = (bf16[128,2048]{1,0:T(8,128)(2,1)S(1)}, bf16[128,2048]{1,0:T(8,128)(2,1)}, u32[]{:S(2)}) copy-start(bf16[128,2048]{1,0:T(8,128)(2,1)} %copy-done.1) | copy-start | bytes 1572868
  370.5 7.2 %copy-start.11 = (s32[128,6]{0,1:T(8,128)S(1)}, s32[128,6]{0,1:T(8,128)}, u32[]{:S(2)}) copy-start(s32[128,6]{0,1:T(8,128)} %param.28) | copy-start | bytes 9220
  370.5 83.2 %all-to-all-start.1 = ((bf16[16,60,2048]{2,1,0:T(8,128)(2,1)}), bf16[16,60,2048]{2,1,0:T(8,128)(2,1)}, u32[]{:S(2)}, u32[]{:S(2)}) async-start(bf16[16,60,2048]{2,1,0:T(8,128)(2,1)} %reshape.143), calls=%async_computation.1 | async-start | bytes 8388608 | tf_op jit(solution)/shard_map/all_to_all | solution.py:39
  376.0 143.8 %reduce-scatter.2.cloned.1.call-start = ((), (), s32[]{:S(2)}) async-start(), calls=%async_computation.4 | async-start | bytes 786432 | tf_op jit(solution)/shard_map/reduce_scatter | solution.py:142
  487.7 32.1 %copy-start.3 = (bf16[128,2048]{1,0:T(8,128)(2,1)S(1)}, bf16[128,2048]{1,0:T(8,128)(2,1)}, u32[]{:S(2)}) copy-start(bf16[128,2048]{1,0:T(8,128)(2,1)} %all-reduce.3.cloned.1.call-done) | copy-start | bytes 1572868
Sparse Core Ops, SparseCore 0:
  13.7 129.9 all-gather.2
  161.8 66.8 all-reduce.2
  491.2 28.5 reduce-scatter.1
where the time goes:
time: 530 us; the launch traced here: 528 us
  waiting for transfers between devices  250 us (47%)
  blocking collectives  122 us (23%)
  local copies, waits for them, and re-layouts  80.5 us (15%)
  matrix products  35.4 us (7%)
  other arithmetic  21.1 us (4%)
  between operations  13.4 us (3%)
  starting transfers between devices  5.79 us (1%)
    all_to_all x1, blocking collectives, per_device(): lax.all_to_all(outgoing, 'ctx', split_axis=0, concat_axis=0, tiled=True)  98 us
    all_gather x1, waiting for transfers between devices, entering_2(): gathered = jax.tree.map(lambda a: lax.all_gather(a, axis), part)  81.7 us
    all_to_all x1, waiting for transfers between devices, run_rows(): lax.all_to_all(shaped, 'ctx', split_axis=0, concat_axis=0, tiled=True)  75.9 us
    psum x1, waiting for transfers between devices, per_device(): hidden_all = lax.psum(with_stream.astype(jnp.bfloat16), 'exp')  63.5 us
    gather x6, local copies, waits for them, and re-layouts, per_device(): picked_rows = flat_back[slot_rows[:, choice_number]].astype(jnp.float32)  29.2 us
    reduce_scatter x1, waiting for transfers between devices, per_device(): lax.psum_scatter(moe_part.astype(jnp.bfloat16), 'exp', scatter_dimension=...  28.7 us
    all_gather x1, blocking collectives, entering_2(): gathered = jax.tree.map(lambda a: lax.all_gather(a, axis), part)  24 us
    dot_general x1, matrix products, run_rows(): jnp.dot(active, w_down[0], preferred_element_type=jnp.float32)  12.2 us
  transfers between devices with their start and end apart: 4, of which 4 were waited for; matrix products, arithmetic and copies ran while one was open for 6% of the time, Pallas kernels for 0%

commit v1 on v0

v1 whole, which is shorter than its diff:
```python
import functools

import jax
import jax.numpy as jnp
from jax import lax
from jax.experimental import pallas as pl
from jax.experimental.pallas import tpu as pltpu
from jax.sharding import PartitionSpec as P

P_SIZE = 64
N = 128
PLANE = 4


def move(value, partner):
    return lax.ppermute(value, "ctx", [(i, partner(i)) for i in range(lax.axis_size("ctx"))])


def as_rows(flat, width):
    tile = 8 * width
    return jnp.pad(flat, (0, -flat.shape[0] % tile)).reshape(-1, width)


def chain_kernel(pairs, out):
    count, share, width = out.shape
    line = lax.broadcasted_iota(jnp.int32, (share, width), 0)
    lane = lax.broadcasted_iota(jnp.int32, (share, width), 1)
    entering = jnp.zeros((share, width), jnp.float32)
    for pair in range(count):
        out[pair] = entering
        logs = jnp.where(line == lane, pairs[pair, share : share + 1, :], 0.0)
        decay = jnp.exp(jnp.sum(logs, axis=1, keepdims=True))
        entering = decay * entering + pairs[pair, :share]


def prefix_states(state, log_total, extra):
    size = lax.axis_size("ctx")
    odd = lax.axis_index("ctx") % 2 == 1
    rows, width = state.shape
    half = rows // 2
    share = rows // size
    extra_rows = extra.shape[0]
    row_log = jnp.repeat(log_total, rows // log_total.shape[0])

    def halves(array):
        return array[:half], array[half:]

    def pick(flag, first, second):
        return jnp.where(flag, second, first)

    low, high = halves(state)
    log_low, log_high = halves(row_log)
    kept, given = pick(odd, low, high), pick(odd, high, low)
    kept_log, given_log = pick(odd, log_low, log_high), pick(odd, log_high, log_low)
    log_rows = as_rows(given_log, width)
    got = move(jnp.concatenate([given, log_rows, extra], axis=0), lambda i: i ^ 1)
    got_log = got[half : half + log_rows.shape[0]].reshape(-1)[:half]
    got_extra = got[half + log_rows.shape[0] :]
    got = got[:half]
    first, second = pick(odd, kept, got), pick(odd, got, kept)
    first_log, second_log = pick(odd, kept_log, got_log), pick(odd, got_log, kept_log)
    pair_extra = jnp.concatenate([pick(odd, extra, got_extra), pick(odd, got_extra, extra)], axis=0)
    pair_state = jnp.exp(second_log)[:, None] * first + second
    pair_log = (first_log + second_log).reshape(size // 2, 1, share)
    pair_log = jnp.pad(pair_log, ((0, 0), (0, 7), (0, width - share)))
    pair_extra = jnp.broadcast_to(pair_extra[None], (size // 2, 2 * extra_rows, width))
    sent = jnp.concatenate(
        [pair_state.reshape(size // 2, share, width), pair_log, pair_extra], axis=1
    )
    groups = [[i for i in range(size) if i % 2 == k] for k in range(2)]

    def exchange(array):
        return lax.all_to_all(
            array, "ctx", split_axis=0, concat_axis=0, axis_index_groups=groups, tiled=True
        )

    pairs = exchange(sent)
    found = pl.pallas_call(
        chain_kernel, out_shape=jax.ShapeDtypeStruct((size // 2, share, width), jnp.float32)
    )(pairs)
    into_first = exchange(found).reshape(half, width)
    into_second = jnp.exp(first_log)[:, None] * into_first + first
    mine, other = pick(odd, into_first, into_second), pick(odd, into_second, into_first)
    back = move(other, lambda i: i ^ 1)
    return mine, back, pairs[:, share + 8 :].reshape(size, extra_rows, width)


def after(value, *earlier):
    return lax.optimization_barrier((value, *earlier))[0] if earlier else value


def expert_kernel(planes, top, place, *refs):
    sources, refs = refs[: 4 * planes], refs[4 * planes :]
    ids, moe_gain, router, hbm_weights, refs = refs[0], refs[1], refs[2], refs[3:9], refs[9:]
    hbm_outs, refs = refs[: 4 * planes], refs[4 * planes :]
    pieces, rows, acts, outs, weights, came, loaded, left_out = refs
    count, half = sources[0].shape
    width = 2 * half
    inputs = [
        pltpu.make_async_copy(source, pieces.at[i], came.at[i]) for i, source in enumerate(sources)
    ]
    units = hbm_weights[0].shape[0]
    loads = [
        pltpu.make_async_copy(
            source.at[pl.ds(part * units // 2, units // 2)],
            weights.at[i, pl.ds(part * units // 2, units // 2)],
            loaded.at[2 * i + part],
        )
        for i, source in enumerate(hbm_weights)
        for part in range(2)
    ]
    for copy in inputs:
        copy.start()
    own = pl.multiple_of(place[1] * half, half)
    rest = pl.multiple_of((1 - place[1]) * half, half)
    gain_own, gain_rest = moe_gain[:, pl.ds(own, half)], moe_gain[:, pl.ds(rest, half)]
    contract = (((1,), (1,)), ((), ()))
    for plane in range(planes):
        for line in range(2):
            inputs[4 * plane + 2 * line].wait()
            inputs[4 * plane + 2 * line + 1].wait()
            if plane == 0:
                loads[2 * line].start()
                loads[2 * line + 1].start()
            left = pieces[4 * plane + 2 * line].astype(jnp.float32)
            right = pieces[4 * plane + 2 * line + 1].astype(jnp.float32)
            total = jnp.sum(left * left, axis=1, keepdims=True) + jnp.sum(
                right * right, axis=1, keepdims=True
            )
            scale = lax.rsqrt(total / width + 1e-06)
            where = pl.ds((2 * plane + line) * count, count)
            rows[where, pl.ds(own, half)] = (left * scale * gain_own).astype(jnp.bfloat16)
            rows[where, pl.ds(rest, half)] = (right * scale * gain_rest).astype(jnp.bfloat16)

    def load(index):
        for part in range(2 * index, 2 * index + 2):
            loads[part].wait()
            if part + 4 < len(loads):
                loads[part + 4].start()

    logits = lax.dot_general(
        router[...], rows[...], (((0,), (1,)), ((), ())), preferred_element_type=jnp.float32
    )
    score = jax.nn.sigmoid(logits)
    experts = score.shape[0]
    number = lax.broadcasted_iota(jnp.int32, (experts, count), 0).astype(jnp.float32)
    shares = []
    for block in range(2 * planes):
        chosen = number == ids[block, 0:1, :]
        for choice in range(1, top):
            chosen = chosen | (number == ids[block, choice : choice + 1, :])
        picked = jnp.where(chosen, score[:, block * count : (block + 1) * count], 0.0)
        shares.append(picked / jnp.sum(picked, axis=0, keepdims=True))
    line = lax.broadcasted_iota(jnp.int32, (count, count), 0)
    lane = lax.broadcasted_iota(jnp.int32, (count, count), 1)
    expert = lax.broadcasted_iota(jnp.int32, (experts, count), 0)
    for which in range(2):
        columns = []
        for share in shares:
            row = jnp.sum(
                jnp.where(expert == place[2 * which], share, 0.0), axis=0, keepdims=True
            )
            columns.append(jnp.sum(jnp.where(line == lane, row, 0.0), axis=1, keepdims=True))
        gate = jnp.concatenate(columns, axis=0)
        load(3 * which)
        gate_proj = lax.dot_general(
            rows[...], weights[3 * which], contract, preferred_element_type=jnp.float32
        )
        load(3 * which + 1)
        up_proj = lax.dot_general(
            rows[...], weights[3 * which + 1], contract, preferred_element_type=jnp.float32
        )
        load(3 * which + 2)
        active = gate_proj / (1.0 + jnp.exp(-gate_proj)) * up_proj
        acts[which] = (active * gate).astype(jnp.bfloat16)
    sends = []
    for side, start in ((1, rest), (0, own)):
        part = jnp.dot(acts[0], weights[2, :, pl.ds(start, half)], preferred_element_type=jnp.float32)
        part += jnp.dot(
            acts[1], weights[5, :, pl.ds(start, half)], preferred_element_type=jnp.float32
        )
        part = part.astype(jnp.bfloat16)
        for plane in range(planes):
            for line in (1, 0):
                index = 4 * plane + 2 * line + side
                first = (2 * plane + line) * count
                outs[index] = part[first : first + count]
                send = pltpu.make_async_copy(outs.at[index], hbm_outs[index], left_out.at[index])
                send.start()
                sends.append(send)
    for send in sends:
        send.wait()


def run_expert(place, pieces, ids, top, moe_gain, router, weights):
    count, half = pieces[0].shape
    planes = len(pieces) // 4
    units, width = weights[0].shape
    rows = 2 * planes * count
    hbm = pl.BlockSpec(memory_space=pltpu.HBM)
    vmem = pl.BlockSpec(memory_space=pltpu.VMEM)
    return pl.pallas_call(
        functools.partial(expert_kernel, planes, top),
        out_shape=[jax.ShapeDtypeStruct((count, half), jnp.bfloat16)] * (4 * planes),
        in_specs=[pl.BlockSpec(memory_space=pltpu.SMEM)]
        + [hbm] * (4 * planes)
        + [vmem] * 3
        + [hbm] * 6,
        out_specs=[hbm] * (4 * planes),
        scratch_shapes=[
            pltpu.VMEM((4 * planes, count, half), jnp.bfloat16),
            pltpu.VMEM((rows, width), jnp.bfloat16),
            pltpu.VMEM((2, rows, units), jnp.bfloat16),
            pltpu.VMEM((4 * planes, count, half), jnp.bfloat16),
            pltpu.VMEM((6, units, width), jnp.bfloat16),
            pltpu.SemaphoreType.DMA((4 * planes,)),
            pltpu.SemaphoreType.DMA((12,)),
            pltpu.SemaphoreType.DMA((4 * planes,)),
        ],
        compiler_params=pltpu.CompilerParams(vmem_limit_bytes=42 * 2**20),
        cost_estimate=pl.CostEstimate(
            flops=2 * 6 * rows * width * units,
            bytes_accessed=2 * (6 * units * width + 8 * planes * count * half),
            transcendentals=2 * rows * units,
        ),
    )(place, *pieces, ids, moe_gain, router, *weights)


def dense_experts(hidden, every_ids, top, moe_gain, router, weights):
    size = lax.axis_size("ctx")
    planes = size // PLANE
    here, side = lax.axis_index("ctx"), lax.axis_index("exp")
    even = here % 2 == 0

    def flip(value, bit):
        return move(value, lambda i: i ^ bit)

    def across(value):
        return lax.ppermute(value, "exp", [(0, 1), (1, 0)])

    def diagonal(value):
        pairs = [
            (i * 2 + x, i * 2 + 1 - x if i % 2 == 0 else (i ^ 2) * 2 + x)
            for i in range(size)
            for x in range(2)
        ]
        return lax.ppermute(value, ("ctx", "exp"), pairs)

    def shift(value, planes_on):
        return move(value, lambda i: (i + PLANE * planes_on) % size)

    weights = [*weights, *(flip(weight, 1) for weight in weights)]
    groups = [[0,1],[2,3]]
    place = jnp.stack([here, side, here ^ 1]).astype(jnp.int32)
    gain = moe_gain[None]
    ties = [(('x', 0), ('z', 3)), (('y', 0), ('z', 3)), (('K', 0), ('turn', 3)), (('z', 2), ('turn', 0)), (('z', 1), ('turn', 0)), (('tox', 0), ('K', 1)), (('tox', 1), ('K', 1))]
    memo = {}

    def get(name, index):
        key = (name, index)
        if key not in memo:
            memo[key] = make(name, index)
        return memo[key]

    def tied(value, name, index):
        return after(value, *[get(*source) for source, target in ties if target == (name, index)])

    def make(name, p):
        if name == "z":
            return hidden if p == 0 else shift(tied(hidden, name, p), -p)
        if name == "x":
            return across(tied(get("z", p), name, p))
        if name == "y":
            return flip(tied(get("z", p), name, p), 2)
        if name == "turn":
            return tied(jnp.where(even, get("y", p), get("x", p)), name, p)
        if name == "diag":
            return diagonal(get("turn", p))
        if name == "outs":
            group = groups[p]
            order = jnp.stack(
                [
                    (here // PLANE + plane) % planes * PLANE + ((here % PLANE) ^ flips)
                    for plane in group
                    for flips in (0, 2)
                ]
            )
            pieces = [get(part, plane) for plane in group for part in ("z", "x", "y", "diag")]
            return run_expert(
                place, pieces, every_ids[order], top, tied(gain, "K", p), router, weights
            )
        if name == "K":
            return get("outs", p)[3]
        group = [g for g in range(len(groups)) if p in groups[g]][0]
        kept, to_x, to_y, corner = get("outs", group)[4 * groups[group].index(p) :][:4]
        if name == "rdiag":
            return diagonal(tied(corner, name, p))
        zero = jnp.zeros_like(corner)
        if name == "toy":
            return to_y + jnp.where(even, get("rdiag", p), zero)
        if name == "tox":
            return to_x + jnp.where(even, zero, get("rdiag", p))
        if name == "sum":
            value = (
                kept.astype(jnp.float32)
                + across(get("tox", p)).astype(jnp.float32)
                + flip(get("toy", p), 2).astype(jnp.float32)
            )
            return value if p == 0 else value.astype(jnp.bfloat16)
        if name == "back":
            value = get("sum", p)
            return value if p == 0 else shift(value, p).astype(jnp.float32)

    total = hidden.astype(jnp.float32)
    for plane in range(planes):
        total = total + get("back", plane)
    return total.astype(jnp.bfloat16)


def run_rows(pieces, w_gate, w_up, w_down):
    row_count = pieces.shape[0] * pieces.shape[1]
    flattened = pieces.reshape(row_count, pieces.shape[2])
    contract = (((1,), (1,)), ((), ()))
    gate_proj = lax.dot_general(flattened, w_gate[0], contract, preferred_element_type=jnp.float32)
    up_proj = lax.dot_general(flattened, w_up[0], contract, preferred_element_type=jnp.float32)
    active = (jax.nn.silu(gate_proj) * up_proj).astype(jnp.bfloat16)
    partial_value = jnp.dot(active, w_down[0], preferred_element_type=jnp.float32).astype(
        jnp.bfloat16
    )
    full_width = partial_value.shape[1]
    shaped = partial_value.reshape(pieces.shape[0], pieces.shape[1], full_width)
    return lax.all_to_all(shaped, "ctx", split_axis=0, concat_axis=0, tiled=True)


def columns_of(rows):
    pad = jnp.zeros((-rows.shape[0] % 128, rows.shape[1]), rows.dtype)
    return jnp.concatenate([rows, pad], axis=0).T if pad.shape[0] else rows.T


def state_kernel(step, rate, x, b, state, running):
    heads, count = step.shape
    groups = b.shape[1] // N
    per_group = heads // groups
    wide = per_group * P_SIZE
    total = -step[...] * rate[...]
    lane = lax.broadcasted_iota(jnp.int32, (heads, count), 1)
    hop = 1
    while hop < count:
        total = total + jnp.where(lane >= hop, pltpu.roll(total, hop, 1), 0.0)
        hop *= 2
    running[...] = total
    weight = jnp.exp(total[:, count - 1 :] - total) * step[...]
    for group in range(groups):
        turned = x[:, group * wide : (group + 1) * wide].astype(jnp.float32).T
        carried = jnp.concatenate(
            [
                turned[q * P_SIZE : (q + 1) * P_SIZE]
                * weight[group * per_group + q : group * per_group + q + 1]
                for q in range(per_group)
            ],
            axis=0,
        ).astype(jnp.bfloat16)
        state[group * wide : (group + 1) * wide] = jnp.dot(
            carried, b[:, group * N : (group + 1) * N], preferred_element_type=jnp.float32
        )


def inner_kernel(step, running, x, b, c, inner):
    heads, count = step.shape
    groups = b.shape[1] // N
    per_group = heads // groups
    total = running[...]
    columns = columns_of(total)
    line = lax.broadcasted_iota(jnp.int32, (count, count), 0)
    lane = lax.broadcasted_iota(jnp.int32, (count, count), 1)
    first = lax.broadcasted_iota(jnp.int32, (count, 2 * P_SIZE), 1) < P_SIZE
    for group in range(groups):
        where = slice(group * N, (group + 1) * N)
        scores = lax.dot_general(
            c[:, where], b[:, where], (((1,), (1,)), ((), ())), preferred_element_type=jnp.float32
        )
        scores = jnp.where(line >= lane, scores, 0.0)
        for pair in range(per_group // 2):
            head = group * per_group + 2 * pair
            mixing = []
            for h in (head, head + 1):
                spread = columns[:, h : h + 1] - total[h : h + 1]
                decay = jnp.exp(jnp.where(line >= lane, spread, 0.0))
                mixing.append((decay * scores * step[h : h + 1]).astype(jnp.bfloat16))
            both = x[:, head * P_SIZE : (head + 2) * P_SIZE].astype(jnp.float32)
            apart = jnp.concatenate(
                [jnp.where(first, both, 0.0), jnp.where(first, 0.0, both)], axis=0
            )
            inner[:, head * P_SIZE : (head + 2) * P_SIZE] = jnp.dot(
                jnp.concatenate(mixing, axis=1),
                apart.astype(jnp.bfloat16),
                preferred_element_type=jnp.float32,
            )


def mixer_kernel(
    place, mine, back, c, inner, running, z, gain, weight, stream, own, theirs, high, low, normed
):
    heads, count = running.shape
    groups = c.shape[1] // N
    per_group = heads // groups
    wide = per_group * P_SIZE
    half = mine.shape[0]
    odd = place[0] % 2
    for part in range(2):
        value = jnp.where(odd == part, mine[...], back[...])
        rounded = value.astype(jnp.bfloat16)
        high[part * half : (part + 1) * half] = rounded
        low[part * half : (part + 1) * half] = (value - rounded.astype(jnp.float32)).astype(
            jnp.bfloat16
        )
    growth = columns_of(jnp.exp(running[...]))
    first = lax.broadcasted_iota(jnp.int32, (count, 2 * P_SIZE), 1) < P_SIZE
    contract = (((1,), (1,)), ((), ()))
    for group in range(groups):
        where = slice(group * wide, (group + 1) * wide)
        reads = c[:, group * N : (group + 1) * N]
        carried = lax.dot_general(
            reads, high[where], contract, preferred_element_type=jnp.float32
        ) + lax.dot_general(reads, low[where], contract, preferred_element_type=jnp.float32)
        heads_in = range(group * per_group, (group + 1) * per_group, 2)
        scale = jnp.concatenate(
            [jnp.where(first, growth[:, h : h + 1], growth[:, h + 1 : h + 2]) for h in heads_in],
            axis=1,
        )
        gate = z[:, where].astype(jnp.float32)
        gated = (inner[:, where] + scale * carried) * (gate / (1.0 + jnp.exp(-gate)))
        mean = jnp.sum(gated * gated, axis=1, keepdims=True) / wide
        normed[:, where] = (gated * lax.rsqrt(mean + 1e-05) * gain[:, where]).astype(jnp.bfloat16)
    width = stream.shape[1]
    shares = theirs.shape[0] + 1
    for step in range(shares - 1, -1, -1):
        start = pl.multiple_of(lax.rem(place[1] + step, shares) * width, width)
        part = jnp.dot(
            normed[...], weight[:, pl.ds(start, width)], preferred_element_type=jnp.float32
        )
        if step:
            theirs[step - 1] = part.astype(jnp.bfloat16)
        else:
            own[...] = part + stream[...].astype(jnp.float32)


def per_device(
    ssm_input,
    gate_input,
    b_input,
    c_input,
    step_size,
    decay_rate,
    norm_gain,
    out_weight,
    stream,
    moe_gain,
    router,
    expert_ids,
    w_gate,
    w_up,
    w_down,
):
    token_count, inner_width = ssm_input.shape
    head_count = step_size.shape[0]
    slice_width = stream.shape[1]
    expert_count = router.shape[1]
    top_count = expert_ids.shape[1]
    exp_size = lax.axis_size("exp")
    capacity = max(
        2, token_count * top_count // expert_count + token_count * top_count // (4 * expert_count)
    )
    vmem = pl.BlockSpec(memory_space=pltpu.VMEM)
    wide = jax.ShapeDtypeStruct((token_count, inner_width), jnp.float32)
    state, running = pl.pallas_call(
        state_kernel,
        out_shape=[
            jax.ShapeDtypeStruct((inner_width, N), jnp.float32),
            jax.ShapeDtypeStruct(step_size.shape, jnp.float32),
        ],
        in_specs=[vmem] * 4,
        out_specs=[vmem] * 2,
        compiler_params=pltpu.CompilerParams(vmem_limit_bytes=16 * 2**20),
    )(step_size, decay_rate[:, None], ssm_input, b_input)
    id_rows = jnp.pad(expert_ids.T.astype(jnp.float32), ((0, -expert_ids.shape[1] % 8), (0, 0)))
    mine, back, every_ids = prefix_states(state, running[:, -1], id_rows)
    inner = pl.pallas_call(
        inner_kernel,
        out_shape=wide,
        in_specs=[vmem] * 5,
        out_specs=vmem,
        compiler_params=pltpu.CompilerParams(vmem_limit_bytes=16 * 2**20),
    )(step_size, running, ssm_input, b_input, c_input)
    place = jnp.stack([lax.axis_index("ctx"), lax.axis_index("exp")]).astype(jnp.int32)
    hidden_own, theirs = pl.pallas_call(
        mixer_kernel,
        out_shape=[
            jax.ShapeDtypeStruct(stream.shape, jnp.float32),
            jax.ShapeDtypeStruct((exp_size - 1, *stream.shape), jnp.bfloat16),
        ],
        in_specs=[pl.BlockSpec(memory_space=pltpu.SMEM)] + [vmem] * 9,
        out_specs=[vmem] * 2,
        scratch_shapes=[
            pltpu.VMEM((inner_width, N), jnp.bfloat16),
            pltpu.VMEM((inner_width, N), jnp.bfloat16),
            pltpu.VMEM((token_count, inner_width), jnp.bfloat16),
        ],
        compiler_params=pltpu.CompilerParams(vmem_limit_bytes=24 * 2**20),
    )(place, mine, back, c_input, inner, running, gate_input, norm_gain[None], out_weight, stream)
    for step in range(1, exp_size):
        ring = [(i, (i + step) % exp_size) for i in range(exp_size)]
        sent = lax.ppermute(theirs[step - 1], "exp", ring)
        hidden_own = hidden_own + sent.astype(jnp.float32)
    hidden_own = hidden_own.astype(jnp.bfloat16)
    every_token = token_count * lax.axis_size("ctx")
    if exp_size == 2 and every_token <= 3 * expert_count * capacity:
        return dense_experts(
            hidden_own,
            every_ids,
            top_count,
            moe_gain,
            router,
            (w_gate[0], w_up[0], w_down[0]),
        )
    hidden_all = lax.all_gather(hidden_own, "exp", axis=1, tiled=True)
    hidden_f = hidden_all.astype(jnp.float32)
    mean_h = jnp.mean(hidden_f * hidden_f, axis=1, keepdims=True)
    sent_rows = (hidden_f * lax.rsqrt(mean_h + 1e-06) * moe_gain).astype(jnp.bfloat16)
    logits = jnp.dot(sent_rows, router, preferred_element_type=jnp.float32)
    sigmoid_score = jax.nn.sigmoid(logits)
    expert_range = jnp.arange(expert_count, dtype=jnp.int32)
    matches = expert_ids[:, :, None] == expert_range
    picked = jnp.sum(jnp.where(matches, sigmoid_score[:, None, :], 0.0), axis=2)
    gates = picked / jnp.sum(picked, axis=1, keepdims=True)
    flat_ids = expert_ids.reshape(-1)
    one_hot = (flat_ids[:, None] == expert_range).astype(jnp.int32)
    slot_index = jnp.sum((jnp.cumsum(one_hot, axis=0) - one_hot) * one_hot, axis=1)
    target = flat_ids * capacity + slot_index
    token_of = jnp.arange(token_count * top_count, dtype=jnp.int32) // top_count
    source_row = (
        jnp.full((expert_count * capacity,), token_count, jnp.int32).at[target].set(token_of)
    )
    padded = jnp.concatenate([sent_rows, jnp.zeros((1, sent_rows.shape[1]), jnp.bfloat16)], axis=0)
    outgoing = padded[source_row].reshape(expert_count, capacity, sent_rows.shape[1])
    returned = run_rows(
        lax.all_to_all(outgoing, "ctx", split_axis=0, concat_axis=0, tiled=True),
        w_gate,
        w_up,
        w_down,
    )
    back_width = returned.shape[2]
    flat_back = returned.reshape(expert_count * capacity, back_width)
    slot_rows = target.reshape(token_count, top_count)
    moe_part = jnp.zeros((token_count, back_width), jnp.float32)
    for choice_number in range(top_count):
        picked_rows = flat_back[slot_rows[:, choice_number]].astype(jnp.float32)
        moe_part = moe_part + gates[:, choice_number][:, None] * picked_rows
    moe_sum = lax.psum_scatter(
        moe_part.astype(jnp.bfloat16), "exp", scatter_dimension=1, tiled=True
    ).astype(jnp.float32)
    return (hidden_own.astype(jnp.float32) + moe_sum).astype(jnp.bfloat16)


def solution(mesh):
    in_specs = (
        P("ctx", "exp"),
        P("ctx", "exp"),
        P("ctx", "exp"),
        P("ctx", "exp"),
        P("exp", "ctx"),
        P("exp"),
        P("exp"),
        P("exp", None),
        P("ctx", "exp"),
        P(),
        P(),
        P("ctx", None),
        P("ctx", "exp", None),
        P("ctx", "exp", None),
        P("ctx", "exp", None),
    )
    out_specs = P("ctx", "exp")
    return jax.shard_map(
        per_device, mesh=mesh, in_specs=in_specs, out_specs=out_specs, check_vma=False
    )
```

time: 530 us -> 209 us (0.39)
  waiting for transfers between devices: 250 us -> 86.3 us
  blocking collectives: 122 us -> 24.6 us
  local copies, waits for them, and re-layouts: 80.5 us -> 13.3 us
  Pallas kernels: 0 us -> 44.3 us
  matrix products: 35.4 us -> 0 us
  starting transfers between devices: 5.79 us -> 34.5 us
  other arithmetic: 21.1 us -> 5.06 us
  between operations: 13.4 us -> 0.33 us
    all_gather x1 -> x0, waiting for transfers between devices: 81.7 us -> none  [entering_2(): gathered = jax.tree.map(lambda a: lax.all_gather(a, axis), part)]
    all_to_all x1, blocking collectives: 98 us -> 24.6 us  [exchange(): lax.all_to_all(array, 'ctx', split_axis=0, concat_axis=0, axis_index_grou...]
    ppermute x0 -> x36, waiting for transfers between devices: none -> 72.9 us  [the longest x19 35.6 us: move(): lax.ppermute(value, 'ctx', [(i, partner(i)) for i in range(lax.axis_size(...]
    psum x1 -> x0, waiting for transfers between devices: 63.5 us -> none  [per_device(): hidden_all = lax.psum(with_stream.astype(jnp.bfloat16), 'exp')]
    all_to_all x1, waiting for transfers between devices: 75.9 us -> 13.4 us  [exchange(): lax.all_to_all(array, 'ctx', split_axis=0, concat_axis=0, axis_index_grou...]
    pallas_call x0 -> x6, Pallas kernels: none -> 44.3 us  [the longest x2 36.6 us: run_expert(): pl.pallas_call(functools.partial(expert_kernel, planes, top), out_shape=[...]
    dot_general x8 -> x0, matrix products: 35.4 us -> none  [the longest x1 12.2 us: run_rows(): jnp.dot(active, w_down[0], preferred_element_type=jnp.float32)]
    gather x7 -> x2, local copies, waits for them, and re-layouts: 35.1 us -> 1.1 us  [make(): every_ids[order]]
  transfers between devices with their start and end apart: 4 -> 37, of which waited for: 4 -> 20; matrix products, arithmetic and copies ran while one was open for 6% -> 3% of each run, Pallas kernels for 0% -> 11%
where the time goes in v1:
time: 209 us; the launch traced here: 208 us
  waiting for transfers between devices  86.3 us (41%)
  Pallas kernels  44.3 us (21%)
  starting transfers between devices  34.5 us (17%)
  blocking collectives  24.6 us (12%)
  local copies, waits for them, and re-layouts  13.3 us (6%)
  other arithmetic  5.06 us (2%)
    pallas_call x2, Pallas kernels, run_expert(): pl.pallas_call(functools.partial(expert_kernel, planes, top), out_shape=[...  36.6 us
    ppermute x19, waiting for transfers between devices, move(): lax.ppermute(value, 'ctx', [(i, partner(i)) for i in range(lax.axis_size(...  35.6 us
    all_to_all x1, blocking collectives, exchange(): lax.all_to_all(array, 'ctx', split_axis=0, concat_axis=0, axis_index_grou...  24.6 us
    ppermute x8, waiting for transfers between devices, diagonal(): return lax.ppermute(value, ('ctx', 'exp'), pairs)  19.7 us
    all_to_all x1, waiting for transfers between devices, exchange(): lax.all_to_all(array, 'ctx', split_axis=0, concat_axis=0, axis_index_grou...  13.4 us
    ppermute x19, starting transfers between devices, move(): lax.ppermute(value, 'ctx', [(i, partner(i)) for i in range(lax.axis_size(...  11.8 us
    ppermute x8, waiting for transfers between devices, across(): return lax.ppermute(value, 'exp', [(0, 1), (1, 0)])  10.8 us
    unnamed x31, local copies, waits for them, and re-layouts  10 us
  transfers between devices with their start and end apart: 37, of which 20 were waited for; matrix products, arithmetic and copies ran while one was open for 3% of the time, Pallas kernels for 11%

profile of v1, /device:TPU:0, one launch (start us, length us, event | category | flops | bytes accessed | tf_op | source)
XLA Modules:
  0.0 208.4 jit_solution(9996095066689038750)
XLA Ops:
  8.1 24.6 %all_to_all.10.pairs = f32[8,152,128]{2,1,0:T(8,128)} all-to-all(f32[8,152,128]{2,1,0:T(8,128)S(1)} %fusion), channel_id=1, replica_groups={{0,4,8,12,16,20,24,28},{2,6,10,14,18,22,26,30},{1,5,9,13,17,21,25,29},{..., dimensions={0} | all-to-all | bytes 1245184 | tf_op jit(solution)/shard_map/all_to_all | solution.py:73
  32.7 2.2 %shard_map.146 = f32[8,128,128]{2,1,0:T(8,128)} custom-call(f32[8,152,128]{2,1,0:T(8,128)} %all_to_all.10.pairs), custom_call_target="tpu_custom_call" | custom-call | tf_op jit(solution)/shard_map/pallas_call | solution.py:78
  34.9 3.5 %all-to-all-start.1 = ((f32[8,128,128]{2,1,0:T(8,128)}), f32[8,128,128]{2,1,0:T(8,128)S(1)}, u32[]{:S(2)}, u32[]{:S(2)}) async-start(f32[8,128,128]{2,1,0:T(8,128)} %shard_map.146), calls=%async_computation.1 | async-start | bytes 1048576 | tf_op jit(solution)/shard_map/all_to_all | solution.py:73
  39.1 13.4 %all-to-all-done.1 = f32[8,128,128]{2,1,0:T(8,128)S(1)} async-done(((f32[8,128,128]{2,1,0:T(8,128)}), f32[8,128,128]{2,1,0:T(8,128)S(1)}, u32[]{:S(2)}, u32[]{:S(2)}) %all-to-all-start.1) | async-done | bytes 524320 | tf_op jit(solution)/shard_map/all_to_all | solution.py:73
  55.6 3.4 %copy-done = bf16[2048,2048]{1,0:T(8,128)(2,1)S(1)} copy-done((bf16[2048,2048]{1,0:T(8,128)(2,1)S(1)}, bf16[2048,2048]{1,0:T(8,128)(2,1)}, u32[]{:S(2)}) %copy-start) | copy-done | bytes 8388632
  59.0 3.3 %shard_map.148 = (f32[128,1024]{1,0:T(8,128)S(1)}, bf16[1,128,1024]{2,1,0:T(8,128)(2,1)S(1)}) custom-call(s32[2]{0:T(128)S(1)} %pad_add_fusion.place, f32[1024,128]{1,0:T(8,128)S(1)} %get-tuple-element.58.mine, f32[1024,128]{1,0:T(8,128)S(1)} %collective-permute-done.1.back, bf16[128,512]{1,0:T(8,128)(2,1)S(1)} %copy-done.3, ...), custom_call_target="tpu_custom_call" | custom-call | tf_op jit(solution)/shard_map/pallas_call | solution.py:496
  63.9 6.9 %collective-permute-done.2 = bf16[128,1024]{1,0:T(8,128)(2,1)S(1)} collective-permute-done((bf16[128,1024]{1,0:T(8,128)(2,1)S(1)}, bf16[128,1024]{1,0:T(8,128)(2,1)S(1)}, u32[]{:S(2)}, u32[]{:S(2)}) %collective-permute-start.2) | collective-permute-done | bytes 262176 | tf_op jit(solution)/shard_map/ppermute | solution.py:513
  73.5 4.9 %collective-permute-done.6.refs_4_ = bf16[128,1024]{1,0:T(8,128)(2,1)S(1)} collective-permute-done((bf16[128,1024]{1,0:T(8,128)(2,1)S(1)}, bf16[128,1024]{1,0:T(8,128)(2,1)S(1)}, u32[]{:S(2)}, u32[]{:S(2)}) %collective-permute-start.6) | collective-permute-done | bytes 262176 | tf_op jit(solution)/shard_map/ppermute | solution.py:16
  80.3 4.6 %collective-permute-done.4.refs_2_ = bf16[128,1024]{1,0:T(8,128)(2,1)S(1)} collective-permute-done((bf16[128,1024]{1,0:T(8,128)(2,1)S(1)}, bf16[128,1024]{1,0:T(8,128)(2,1)S(1)}, u32[]{:S(2)}, u32[]{:S(2)}) %collective-permute-start.4) | collective-permute-done | bytes 262176 | tf_op jit(solution)/shard_map/ppermute | solution.py:16
  86.4 6.2 %collective-permute-done.5.refs_0_ = bf16[128,1024]{1,0:T(8,128)(2,1)S(1)} collective-permute-done((bf16[128,1024]{1,0:T(8,128)(2,1)S(1)}, bf16[128,1024]{1,0:T(8,128)(2,1)S(1)}, u32[]{:S(2)}, u32[]{:S(2)}) %collective-permute-start.5) | collective-permute-done | bytes 262176 | tf_op jit(solution)/shard_map/ppermute | solution.py:16
  95.5 6.4 %collective-permute-done.9.refs_6_ = bf16[128,1024]{1,0:T(8,128)(2,1)S(1)} collective-permute-done((bf16[128,1024]{1,0:T(8,128)(2,1)S(1)}, bf16[128,1024]{1,0:T(8,128)(2,1)S(1)}, u32[]{:S(2)}, u32[]{:S(2)}) %collective-permute-start.9) | collective-permute-done | bytes 262176 | tf_op jit(solution)/shard_map/ppermute | solution.py:16
  108.2 1.9 collective-permute-done.24.refs_4_
  116.3 18.3 %shard_map.149 = (bf16[128,1024]{1,0:T(8,128)(2,1)S(1)}, bf16[128,1024]{1,0:T(8,128)(2,1)S(1)}, bf16[128,1024]{1,0:T(8,128)(2,1)S(1)}, bf16[128,1024]{1,0:T(8,12...) custom-call(s32[3]{0:T(128)S(1)} %pad_add_fusion.1.place, ...), custom_call_target="tpu_custom_call" | custom-call | flops 8858370048 | bytes 21495808 | tf_op jit(solution)/shard_map/pallas_call | solution.py:202
  139.0 2.1 %collective-permute-done.17 = bf16[128,1024]{1,0:T(8,128)(2,1)S(1)} collective-permute-done((bf16[128,1024]{1,0:T(8,128)(2,1)S(1)}, bf16[128,1024]{1,0:T(8,128)(2,1)S(1)}, u32[]{:S(2)}, u32[]{:S(2)}) %collective-permute-start.17) | collective-permute-done | bytes 262176 | tf_op jit(solution)/shard_map/ppermute | solution.py:247
  141.1 5.6 %collective-permute-done.14 = bf16[128,1024]{1,0:T(8,128)(2,1)S(1)} collective-permute-done((bf16[128,1024]{1,0:T(8,128)(2,1)S(1)}, bf16[128,1024]{1,0:T(8,128)(2,1)S(1)}, u32[]{:S(2)}, u32[]{:S(2)}) %collective-permute-start.14) | collective-permute-done | bytes 262176 | tf_op jit(solution)/shard_map/ppermute | solution.py:247
  146.8 2.7 %collective-permute-done.27.refs_7_ = bf16[128,1024]{1,0:T(8,128)(2,1)S(1)} collective-permute-done((bf16[128,1024]{1,0:T(8,128)(2,1)S(1)}, bf16[128,1024]{1,0:T(8,128)(2,1)S(1)}, u32[]{:S(2)}, u32[]{:S(2)}) %collective-permute-start.27) | collective-permute-done | bytes 262176 | tf_op jit(solution)/shard_map/ppermute | solution.py:247
  149.5 18.3 %shard_map.150 = (bf16[128,1024]{1,0:T(8,128)(2,1)S(1)}, bf16[128,1024]{1,0:T(8,128)(2,1)S(1)}, bf16[128,1024]{1,0:T(8,128)(2,1)S(1)}, bf16[128,1024]{1,0:T(8,12...) custom-call(s32[3]{0:T(128)S(1)} %pad_add_fusion.1.place, ...), custom_call_target="tpu_custom_call" | custom-call | flops 8858370048 | bytes 21495808 | tf_op jit(solution)/shard_map/pallas_call | solution.py:202
  172.8 4.3 %collective-permute-done.28 = bf16[128,1024]{1,0:T(8,128)(2,1)S(1)} collective-permute-done((bf16[128,1024]{1,0:T(8,128)(2,1)S(1)}, bf16[128,1024]{1,0:T(8,128)(2,1)S(1)}, u32[]{:S(2)}, u32[]{:S(2)}) %collective-permute-start.28) | collective-permute-done | bytes 262176 | tf_op jit(solution)/shard_map/ppermute | solution.py:247
  177.8 5.0 %collective-permute-done.32 = bf16[128,1024]{1,0:T(8,128)(2,1)S(1)} collective-permute-done((bf16[128,1024]{1,0:T(8,128)(2,1)S(1)}, bf16[128,1024]{1,0:T(8,128)(2,1)S(1)}, u32[]{:S(2)}, u32[]{:S(2)}) %collective-permute-start.32) | collective-permute-done | bytes 262176 | tf_op jit(solution)/shard_map/ppermute | solution.py:247
  183.7 3.8 %collective-permute-done.18 = bf16[128,1024]{1,0:T(8,128)(2,1)S(1)} collective-permute-done((bf16[128,1024]{1,0:T(8,128)(2,1)S(1)}, bf16[128,1024]{1,0:T(8,128)(2,1)S(1)}, u32[]{:S(2)}, u32[]{:S(2)}) %collective-permute-start.18) | collective-permute-done | bytes 262176 | tf_op jit(solution)/shard_map/ppermute | solution.py:239
  188.6 4.6 %collective-permute-done.29 = bf16[128,1024]{1,0:T(8,128)(2,1)S(1)} collective-permute-done((bf16[128,1024]{1,0:T(8,128)(2,1)S(1)}, bf16[128,1024]{1,0:T(8,128)(2,1)S(1)}, u32[]{:S(2)}, u32[]{:S(2)}) %collective-permute-start.29) | collective-permute-done | bytes 262176 | tf_op jit(solution)/shard_map/ppermute | solution.py:239
  193.7 2.3 %collective-permute-done.33 = bf16[128,1024]{1,0:T(8,128)(2,1)S(1)} collective-permute-done((bf16[128,1024]{1,0:T(8,128)(2,1)S(1)}, bf16[128,1024]{1,0:T(8,128)(2,1)S(1)}, u32[]{:S(2)}, u32[]{:S(2)}) %collective-permute-start.33) | collective-permute-done | bytes 262176 | tf_op jit(solution)/shard_map/ppermute | solution.py:239
  199.5 2.4 %collective-permute-done.20 = bf16[128,1024]{1,0:T(8,128)(2,1)S(1)} collective-permute-done((bf16[128,1024]{1,0:T(8,128)(2,1)S(1)}, bf16[128,1024]{1,0:T(8,128)(2,1)S(1)}, u32[]{:S(2)}, u32[]{:S(2)}) %collective-permute-start.20) | collective-permute-done | bytes 262176 | tf_op jit(solution)/shard_map/ppermute | solution.py:16
  201.9 5.5 %collective-permute-done.31 = bf16[128,1024]{1,0:T(8,128)(2,1)S(1)} collective-permute-done((bf16[128,1024]{1,0:T(8,128)(2,1)S(1)}, bf16[128,1024]{1,0:T(8,128)(2,1)S(1)}, u32[]{:S(2)}, u32[]{:S(2)}) %collective-permute-start.31) | collective-permute-done | bytes 262176 | tf_op jit(solution)/shard_map/ppermute | solution.py:16
  (131 shorter events, 52.0 us)
Async XLA Ops:
  34.9 17.5 %all-to-all-start.1 = ((f32[8,128,128]{2,1,0:T(8,128)}), f32[8,128,128]{2,1,0:T(8,128)S(1)}, u32[]{:S(2)}, u32[]{:S(2)}) async-start(f32[8,128,128]{2,1,0:T(8,128)} %shard_map.146), calls=%async_computation.1 | async-start | bytes 1048576 | tf_op jit(solution)/shard_map/all_to_all | solution.py:73
  38.4 64.2 %collective-permute-start.11 = (bf16[704,2048]{1,0:T(8,128)(2,1)}, bf16[704,2048]{1,0:T(8,128)(2,1)}, u32[]{:S(2)}, u32[]{:S(2)}) collective-permute-start(bf16[704,2048]{1,0:T(8,128)(2,1)} %bitcast.47), channel_id=1, source_target_pairs={{0,2},{2,0},{4,6},{6,4},{8,10},{10,8},{12,14},{14,12},{16,18},{18,... | collective-permute-start | bytes 8650760 | tf_op jit(solution)/shard_map/ppermute | solution.py:16
  38.5 68.0 %collective-permute-start.12 = (bf16[704,2048]{1,0:T(8,128)(2,1)}, bf16[704,2048]{1,0:T(8,128)(2,1)}, u32[]{:S(2)}, u32[]{:S(2)}) collective-permute-start(bf16[704,2048]{1,0:T(8,128)(2,1)} %bitcast.50), channel_id=1, source_target_pairs={{0,2},{2,0},{4,6},{6,4},{8,10},{10,8},{12,14},{14,12},{16,18},{18,... | collective-permute-start | bytes 8650760 | tf_op jit(solution)/shard_map/ppermute | solution.py:16
  39.0 68.1 %collective-permute-start.13 = (bf16[704,2048]{1,0:T(8,128)(2,1)}, bf16[704,2048]{1,0:T(8,128)(2,1)}, u32[]{:S(2)}, u32[]{:S(2)}) collective-permute-start(bf16[704,2048]{1,0:T(8,128)(2,1)} %bitcast.61), channel_id=1, source_target_pairs={{0,2},{2,0},{4,6},{6,4},{8,10},{10,8},{12,14},{14,12},{16,18},{18,... | collective-permute-start | bytes 8650760 | tf_op jit(solution)/shard_map/ppermute | solution.py:16
  79.8 12.8 %collective-permute-start.5 = (bf16[128,1024]{1,0:T(8,128)(2,1)S(1)}, bf16[128,1024]{1,0:T(8,128)(2,1)S(1)}, u32[]{:S(2)}, u32[]{:S(2)}) collective-permute-start(bf16[128,1024]{1,0:T(8,128)(2,1)S(1)} %add_convert_fusion.4.refs_0_), channel_id=1, source_target_pairs={{0,16},{2,18},{4,20},{6,22},{8,24},{10,26},{12,28},{14,30},{16,0},... | collective-permute-start | bytes 786440 | tf_op jit(solution)/shard_map/ppermute | solution.py:16
  92.6 9.2 %collective-permute-start.9 = (bf16[128,1024]{1,0:T(8,128)(2,1)S(1)}, bf16[128,1024]{1,0:T(8,128)(2,1)S(1)}, u32[]{:S(2)}, u32[]{:S(2)}) collective-permute-start(bf16[128,1024]{1,0:T(8,128)(2,1)S(1)} %collective-permute-done.6.refs_4_), channel_id=1, source_target_pairs={{0,4},{2,6},{4,0},{6,2},{8,12},{10,14},{12,8},{14,10},{16,20},{18,... | collective-permute-start | bytes 786440 | tf_op jit(solution)/shard_map/ppermute | solution.py:16
  93.9 17.6 %collective-permute-start.7 = (bf16[128,1024]{1,0:T(8,128)(2,1)S(1)}, bf16[128,1024]{1,0:T(8,128)(2,1)S(1)}, u32[]{:S(2)}, u32[]{:S(2)}) collective-permute-start(bf16[128,1024]{1,0:T(8,128)(2,1)S(1)} %broadcast_select_fusion.3), channel_id=1, source_target_pairs={{0,1},{1,0},{2,6},{3,7},{4,5},{5,4},{6,2},{7,3},{8,9},{9,8},{10,14... | collective-permute-start | bytes 786440 | tf_op jit(solution)/shard_map/ppermute | solution.py:247
  102.6 10.1 %collective-permute-start.10 = (bf16[128,1024]{1,0:T(8,128)(2,1)}, bf16[128,1024]{1,0:T(8,128)(2,1)S(1)}, u32[]{:S(2)}, u32[]{:S(2)}) collective-permute-start(bf16[128,1024]{1,0:T(8,128)(2,1)} %broadcast_select_fusion.2), channel_id=1, source_target_pairs={{0,1},{1,0},{2,6},{3,7},{4,5},{5,4},{6,2},{7,3},{8,9},{9,8},{10,14... | collective-permute-start | bytes 786440 | tf_op jit(solution)/shard_map/ppermute | solution.py:247
  106.5 28.8 %collective-permute-start.21 = (bf16[128,1024]{1,0:T(8,128)(2,1)S(1)}, bf16[128,1024]{1,0:T(8,128)(2,1)S(1)}, u32[]{:S(2)}, u32[]{:S(2)}) collective-permute-start(bf16[128,1024]{1,0:T(8,128)(2,1)S(1)} %collective-permute-done.5.refs_0_), channel_id=1, source_target_pairs={{0,1},{1,0},{2,3},{3,2},{4,5},{5,4},{6,7},{7,6},{8,9},{9,8},{10,11... | collective-permute-start | bytes 786440 | tf_op jit(solution)/shard_map/ppermute | solution.py:239
  107.1 28.2 %collective-permute-start.22 = (bf16[128,1024]{1,0:T(8,128)(2,1)S(1)}, bf16[128,1024]{1,0:T(8,128)(2,1)S(1)}, u32[]{:S(2)}, u32[]{:S(2)}) collective-permute-start(bf16[128,1024]{1,0:T(8,128)(2,1)S(1)} %collective-permute-done.5.refs_0_), channel_id=1, source_target_pairs={{0,4},{2,6},{4,0},{6,2},{8,12},{10,14},{12,8},{14,10},{16,20},{18,... | collective-permute-start | bytes 786440 | tf_op jit(solution)/shard_map/ppermute | solution.py:16
  110.0 27.4 %collective-permute-start.25 = (bf16[128,1024]{1,0:T(8,128)(2,1)S(1)}, bf16[128,1024]{1,0:T(8,128)(2,1)S(1)}, u32[]{:S(2)}, u32[]{:S(2)}) collective-permute-start(bf16[128,1024]{1,0:T(8,128)(2,1)S(1)} %collective-permute-done.24.refs_4_), channel_id=1, source_target_pairs={{0,1},{1,0},{2,3},{3,2},{4,5},{5,4},{6,7},{7,6},{8,9},{9,8},{10,11... | collective-permute-start | bytes 786440 | tf_op jit(solution)/shard_map/ppermute | solution.py:239
  111.5 25.9 %collective-permute-start.26 = (bf16[128,1024]{1,0:T(8,128)(2,1)S(1)}, bf16[128,1024]{1,0:T(8,128)(2,1)S(1)}, u32[]{:S(2)}, u32[]{:S(2)}) collective-permute-start(bf16[128,1024]{1,0:T(8,128)(2,1)S(1)} %collective-permute-done.24.refs_4_), channel_id=1, source_target_pairs={{0,4},{2,6},{4,0},{6,2},{8,12},{10,14},{12,8},{14,10},{16,20},{18,... | collective-permute-start | bytes 786440 | tf_op jit(solution)/shard_map/ppermute | solution.py:16
  135.3 11.5 %collective-permute-start.23 = (bf16[128,1024]{1,0:T(8,128)(2,1)S(1)}, bf16[128,1024]{1,0:T(8,128)(2,1)S(1)}, u32[]{:S(2)}, u32[]{:S(2)}) collective-permute-start(bf16[128,1024]{1,0:T(8,128)(2,1)S(1)} %broadcast_select_fusion.1), channel_id=1, source_target_pairs={{0,1},{1,0},{2,6},{3,7},{4,5},{5,4},{6,2},{7,3},{8,9},{9,8},{10,14... | collective-permute-start | bytes 786440 | tf_op jit(solution)/shard_map/ppermute | solution.py:247
  136.8 9.9 %collective-permute-start.14 = (bf16[128,1024]{1,0:T(8,128)(2,1)S(1)}, bf16[128,1024]{1,0:T(8,128)(2,1)S(1)}, u32[]{:S(2)}, u32[]{:S(2)}) collective-permute-start(bf16[128,1024]{1,0:T(8,128)(2,1)S(1)} %get-tuple-element.36), channel_id=1, source_target_pairs={{0,1},{1,0},{2,6},{3,7},{4,5},{5,4},{6,2},{7,3},{8,9},{9,8},{10,14... | collective-permute-start | bytes 786440 | tf_op jit(solution)/shard_map/ppermute | solution.py:247
  137.4 12.1 %collective-permute-start.27 = (bf16[128,1024]{1,0:T(8,128)(2,1)S(1)}, bf16[128,1024]{1,0:T(8,128)(2,1)S(1)}, u32[]{:S(2)}, u32[]{:S(2)}) collective-permute-start(bf16[128,1024]{1,0:T(8,128)(2,1)S(1)} %broadcast_select_fusion), channel_id=1, source_target_pairs={{0,1},{1,0},{2,6},{3,7},{4,5},{5,4},{6,2},{7,3},{8,9},{9,8},{10,14... | collective-permute-start | bytes 786440 | tf_op jit(solution)/shard_map/ppermute | solution.py:247
  167.9 9.3 %collective-permute-start.28 = (bf16[128,1024]{1,0:T(8,128)(2,1)S(1)}, bf16[128,1024]{1,0:T(8,128)(2,1)S(1)}, u32[]{:S(2)}, u32[]{:S(2)}) collective-permute-start(bf16[128,1024]{1,0:T(8,128)(2,1)S(1)} %get-tuple-element.47), channel_id=1, source_target_pairs={{0,1},{1,0},{2,6},{3,7},{4,5},{5,4},{6,2},{7,3},{8,9},{9,8},{10,14... | collective-permute-start | bytes 786440 | tf_op jit(solution)/shard_map/ppermute | solution.py:247
  168.5 14.3 %collective-permute-start.32 = (bf16[128,1024]{1,0:T(8,128)(2,1)S(1)}, bf16[128,1024]{1,0:T(8,128)(2,1)S(1)}, u32[]{:S(2)}, u32[]{:S(2)}) collective-permute-start(bf16[128,1024]{1,0:T(8,128)(2,1)S(1)} %get-tuple-element.51), channel_id=1, source_target_pairs={{0,1},{1,0},{2,6},{3,7},{4,5},{5,4},{6,2},{7,3},{8,9},{9,8},{10,14... | collective-permute-start | bytes 786440 | tf_op jit(solution)/shard_map/ppermute | solution.py:247
  169.9 17.6 %collective-permute-start.18 = (bf16[128,1024]{1,0:T(8,128)(2,1)S(1)}, bf16[128,1024]{1,0:T(8,128)(2,1)S(1)}, u32[]{:S(2)}, u32[]{:S(2)}) collective-permute-start(bf16[128,1024]{1,0:T(8,128)(2,1)S(1)} %get-tuple-element.67), channel_id=1, source_target_pairs={{0,1},{1,0},{2,3},{3,2},{4,5},{5,4},{6,7},{7,6},{8,9},{9,8},{10,11... | collective-permute-start | bytes 786440 | tf_op jit(solution)/shard_map/ppermute | solution.py:239
  170.5 27.3 %collective-permute-start.15 = (bf16[128,1024]{1,0:T(8,128)(2,1)S(1)}, bf16[128,1024]{1,0:T(8,128)(2,1)S(1)}, u32[]{:S(2)}, u32[]{:S(2)}) collective-permute-start(bf16[128,1024]{1,0:T(8,128)(2,1)S(1)} %get-tuple-element.65), channel_id=1, source_target_pairs={{0,1},{1,0},{2,3},{3,2},{4,5},{5,4},{6,7},{7,6},{8,9},{9,8},{10,11... | collective-permute-start | bytes 786440 | tf_op jit(solution)/shard_map/ppermute | solution.py:239
  172.0 16.1 %collective-permute-start.19 = (bf16[128,1024]{1,0:T(8,128)(2,1)S(1)}, bf16[128,1024]{1,0:T(8,128)(2,1)S(1)}, u32[]{:S(2)}, u32[]{:S(2)}) collective-permute-start(bf16[128,1024]{1,0:T(8,128)(2,1)S(1)} %get-tuple-element.66), channel_id=1, source_target_pairs={{0,4},{2,6},{4,0},{6,2},{8,12},{10,14},{12,8},{14,10},{16,20},{18,... | collective-permute-start | bytes 786440 | tf_op jit(solution)/shard_map/ppermute | solution.py:16
  177.2 15.9 %collective-permute-start.29 = (bf16[128,1024]{1,0:T(8,128)(2,1)S(1)}, bf16[128,1024]{1,0:T(8,128)(2,1)S(1)}, u32[]{:S(2)}, u32[]{:S(2)}) collective-permute-start(bf16[128,1024]{1,0:T(8,128)(2,1)S(1)} %get-tuple-element.68), channel_id=1, source_target_pairs={{0,1},{1,0},{2,3},{3,2},{4,5},{5,4},{6,7},{7,6},{8,9},{9,8},{10,11... | collective-permute-start | bytes 786440 | tf_op jit(solution)/shard_map/ppermute | solution.py:239
  182.8 10.7 %collective-permute-start.30 = (bf16[128,1024]{1,0:T(8,128)(2,1)S(1)}, bf16[128,1024]{1,0:T(8,128)(2,1)S(1)}, u32[]{:S(2)}, u32[]{:S(2)}) collective-permute-start(bf16[128,1024]{1,0:T(8,128)(2,1)S(1)} %get-tuple-element.69), channel_id=1, source_target_pairs={{0,4},{2,6},{4,0},{6,2},{8,12},{10,14},{12,8},{14,10},{16,20},{18,... | collective-permute-start | bytes 786440 | tf_op jit(solution)/shard_map/ppermute | solution.py:16
  196.0 11.4 %collective-permute-start.31 = (bf16[128,1024]{1,0:T(8,128)(2,1)S(1)}, bf16[128,1024]{1,0:T(8,128)(2,1)S(1)}, u32[]{:S(2)}, u32[]{:S(2)}) collective-permute-start(bf16[128,1024]{1,0:T(8,128)(2,1)S(1)} %add_convert_fusion.2), channel_id=1, source_target_pairs={{0,16},{2,18},{4,20},{6,22},{8,24},{10,26},{12,28},{14,30},{16,0},... | collective-permute-start | bytes 786440 | tf_op jit(solution)/shard_map/ppermute | solution.py:16
  196.1 11.2 %collective-permute-start.35 = (bf16[128,1024]{1,0:T(8,128)(2,1)S(1)}, bf16[128,1024]{1,0:T(8,128)(2,1)S(1)}, u32[]{:S(2)}, u32[]{:S(2)}) collective-permute-start(bf16[128,1024]{1,0:T(8,128)(2,1)S(1)} %add_convert_fusion.1), channel_id=1, source_target_pairs={{0,24},{2,26},{4,28},{6,30},{8,0},{10,2},{12,4},{14,6},{16,8},{18,... | collective-permute-start | bytes 786440 | tf_op jit(solution)/shard_map/ppermute | solution.py:16
  (28 other events, 444.6 us)

commit v2 on v1

--- a/solution.py
+++ b/solution.py
@@ -85,45 +85,41 @@
     return mine, back, pairs[:, share + 8 :].reshape(size, extra_rows, width)
 
 
-def after(value, *earlier):
-    return lax.optimization_barrier((value, *earlier))[0] if earlier else value
-
-
 def expert_kernel(planes, top, place, *refs):
     sources, refs = refs[: 4 * planes], refs[4 * planes :]
     ids, moe_gain, router, hbm_weights, refs = refs[0], refs[1], refs[2], refs[3:9], refs[9:]
     hbm_outs, refs = refs[: 4 * planes], refs[4 * planes :]
-    pieces, rows, acts, outs, weights, came, loaded, left_out = refs
+    rows, acts, weights, loaded = refs
+    pieces, outs = sources, hbm_outs
+    units = weights.shape[1]
+    loads = [
+        pltpu.make_async_copy(
+            hbm_weights[i].at[pl.ds(part * units // 2, units // 2)],
+            weights.at[i, pl.ds(part * units // 2, units // 2)],
+            loaded.at[2 * i + part],
+        )
+        for i in (0, 1, 3, 4, 2, 5)
+        for part in range(2)
+    ]
+    for copy in loads[:6]:
+        copy.start()
+
+    def load(index):
+        for part in range(2 * index, 2 * index + 2):
+            loads[part].wait()
+            if part + 6 < len(loads):
+                loads[part + 6].start()
+
     count, half = sources[0].shape
     width = 2 * half
-    inputs = [
-        pltpu.make_async_copy(source, pieces.at[i], came.at[i]) for i, source in enumerate(sources)
-    ]
-    units = hbm_weights[0].shape[0]
-    loads = [
-        pltpu.make_async_copy(
-            source.at[pl.ds(part * units // 2, units // 2)],
-            weights.at[i, pl.ds(part * units // 2, units // 2)],
-            loaded.at[2 * i + part],
-        )
-        for i, source in enumerate(hbm_weights)
-        for part in range(2)
-    ]
-    for copy in inputs:
-        copy.start()
     own = pl.multiple_of(place[1] * half, half)
     rest = pl.multiple_of((1 - place[1]) * half, half)
     gain_own, gain_rest = moe_gain[:, pl.ds(own, half)], moe_gain[:, pl.ds(rest, half)]
     contract = (((1,), (1,)), ((), ()))
     for plane in range(planes):
         for line in range(2):
-            inputs[4 * plane + 2 * line].wait()
-            inputs[4 * plane + 2 * line + 1].wait()
-            if plane == 0:
-                loads[2 * line].start()
-                loads[2 * line + 1].start()
-            left = pieces[4 * plane + 2 * line].astype(jnp.float32)
-            right = pieces[4 * plane + 2 * line + 1].astype(jnp.float32)
+            left = pieces[4 * plane + 2 * line][...].astype(jnp.float32)
+            right = pieces[4 * plane + 2 * line + 1][...].astype(jnp.float32)
             total = jnp.sum(left * left, axis=1, keepdims=True) + jnp.sum(
                 right * right, axis=1, keepdims=True
             )
@@ -131,12 +127,6 @@
             where = pl.ds((2 * plane + line) * count, count)
             rows[where, pl.ds(own, half)] = (left * scale * gain_own).astype(jnp.bfloat16)
             rows[where, pl.ds(rest, half)] = (right * scale * gain_rest).astype(jnp.bfloat16)
-
-    def load(index):
-        for part in range(2 * index, 2 * index + 2):
-            loads[part].wait()
-            if part + 4 < len(loads):
-                loads[part + 4].start()
 
     logits = lax.dot_general(
         router[...], rows[...], (((0,), (1,)), ((), ())), preferred_element_type=jnp.float32
@@ -162,18 +152,18 @@
             )
             columns.append(jnp.sum(jnp.where(line == lane, row, 0.0), axis=1, keepdims=True))
         gate = jnp.concatenate(columns, axis=0)
-        load(3 * which)
+        load(2 * which)
         gate_proj = lax.dot_general(
             rows[...], weights[3 * which], contract, preferred_element_type=jnp.float32
         )
-        load(3 * which + 1)
+        load(2 * which + 1)
         up_proj = lax.dot_general(
             rows[...], weights[3 * which + 1], contract, preferred_element_type=jnp.float32
         )
-        load(3 * which + 2)
         active = gate_proj / (1.0 + jnp.exp(-gate_proj)) * up_proj
         acts[which] = (active * gate).astype(jnp.bfloat16)
-    sends = []
+    load(4)
+    load(5)
     for side, start in ((1, rest), (0, own)):
         part = jnp.dot(acts[0], weights[2, :, pl.ds(start, half)], preferred_element_type=jnp.float32)
         part += jnp.dot(
@@ -184,12 +174,7 @@
             for line in (1, 0):
                 index = 4 * plane + 2 * line + side
                 first = (2 * plane + line) * count
-                outs[index] = part[first : first + count]
-                send = pltpu.make_async_copy(outs.at[index], hbm_outs[index], left_out.at[index])
-                send.start()
-                sends.append(send)
-    for send in sends:
-        send.wait()
+                outs[index][...] = part[first : first + count]
 
 
 def run_expert(place, pieces, ids, top, moe_gain, router, weights):
@@ -197,27 +182,22 @@
     planes = len(pieces) // 4
     units, width = weights[0].shape
     rows = 2 * planes * count
-    hbm = pl.BlockSpec(memory_space=pltpu.HBM)
     vmem = pl.BlockSpec(memory_space=pltpu.VMEM)
     return pl.pallas_call(
         functools.partial(expert_kernel, planes, top),
         out_shape=[jax.ShapeDtypeStruct((count, half), jnp.bfloat16)] * (4 * planes),
         in_specs=[pl.BlockSpec(memory_space=pltpu.SMEM)]
-        + [hbm] * (4 * planes)
+        + [vmem] * (4 * planes)
         + [vmem] * 3
-        + [hbm] * 6,
-        out_specs=[hbm] * (4 * planes),
+        + [pl.BlockSpec(memory_space=pltpu.HBM)] * 6,
+        out_specs=[vmem] * (4 * planes),
         scratch_shapes=[
-            pltpu.VMEM((4 * planes, count, half), jnp.bfloat16),
             pltpu.VMEM((rows, width), jnp.bfloat16),
             pltpu.VMEM((2, rows, units), jnp.bfloat16),
-            pltpu.VMEM((4 * planes, count, half), jnp.bfloat16),
             pltpu.VMEM((6, units, width), jnp.bfloat16),
-            pltpu.SemaphoreType.DMA((4 * planes,)),
             pltpu.SemaphoreType.DMA((12,)),
-            pltpu.SemaphoreType.DMA((4 * planes,)),
         ],
-        compiler_params=pltpu.CompilerParams(vmem_limit_bytes=42 * 2**20),
+        compiler_params=pltpu.CompilerParams(vmem_limit_bytes=56 * 2**20),
         cost_estimate=pl.CostEstimate(
             flops=2 * 6 * rows * width * units,
             bytes_accessed=2 * (6 * units * width + 8 * planes * count * half),
@@ -250,70 +230,75 @@
         return move(value, lambda i: (i + PLANE * planes_on) % size)
 
     weights = [*weights, *(flip(weight, 1) for weight in weights)]
-    groups = [[0,1],[2,3]]
+    groups = [[0],[1],[2],[3]]
+    phases = [
+        [("x", 0), ("y", 0)],
+        [("diag", 0), ("z", 1)],
+        [("K", 0), ("x", 1), ("y", 1), ("z", 2)],
+        [("diag", 1), ("x", 2), ("y", 2), ("z", 3)],
+        [("K", 1), ("x", 3), ("y", 3), ("diag", 2), ("rdiag", 0)],
+        [("K", 2), ("diag", 3), ("rx", 0), ("ry", 0), ("rdiag", 1)],
+        [("K", 3), ("rx", 1), ("ry", 1), ("rdiag", 2)],
+        [("rx", 2), ("ry", 2), ("rdiag", 3), ("rz", 1)],
+        [("rx", 3), ("ry", 3), ("rz", 2)],
+        [("rz", 3)],
+    ]
     place = jnp.stack([here, side, here ^ 1]).astype(jnp.int32)
-    gain = moe_gain[None]
-    ties = [(('x', 0), ('z', 3)), (('y', 0), ('z', 3)), (('K', 0), ('turn', 3)), (('z', 2), ('turn', 0)), (('z', 1), ('turn', 0)), (('tox', 0), ('K', 1)), (('tox', 1), ('K', 1))]
-    memo = {}
-
-    def get(name, index):
-        key = (name, index)
-        if key not in memo:
-            memo[key] = make(name, index)
-        return memo[key]
-
-    def tied(value, name, index):
-        return after(value, *[get(*source) for source, target in ties if target == (name, index)])
-
-    def make(name, p):
+    done = {("z", 0): hidden}
+
+    def operands(name, p):
         if name == "z":
-            return hidden if p == 0 else shift(tied(hidden, name, p), -p)
-        if name == "x":
-            return across(tied(get("z", p), name, p))
-        if name == "y":
-            return flip(tied(get("z", p), name, p), 2)
-        if name == "turn":
-            return tied(jnp.where(even, get("y", p), get("x", p)), name, p)
+            return [done["z", 0]]
+        if name in ("x", "y"):
+            return [done["z", p]]
         if name == "diag":
-            return diagonal(get("turn", p))
-        if name == "outs":
-            group = groups[p]
-            order = jnp.stack(
-                [
-                    (here // PLANE + plane) % planes * PLANE + ((here % PLANE) ^ flips)
-                    for plane in group
-                    for flips in (0, 2)
-                ]
-            )
-            pieces = [get(part, plane) for plane in group for part in ("z", "x", "y", "diag")]
-            return run_expert(
-                place, pieces, every_ids[order], top, tied(gain, "K", p), router, weights
-            )
+            return [jnp.where(even, done["y", p], done["x", p])]
         if name == "K":
-            return get("outs", p)[3]
+            return [done[part, q] for q in groups[p] for part in ("z", "x", "y", "diag")]
         group = [g for g in range(len(groups)) if p in groups[g]][0]
-        kept, to_x, to_y, corner = get("outs", group)[4 * groups[group].index(p) :][:4]
+        kept, to_x, to_y, corner = done["K", group][4 * groups[group].index(p) :][:4]
         if name == "rdiag":
-            return diagonal(tied(corner, name, p))
+            return [corner]
         zero = jnp.zeros_like(corner)
-        if name == "toy":
-            return to_y + jnp.where(even, get("rdiag", p), zero)
-        if name == "tox":
-            return to_x + jnp.where(even, zero, get("rdiag", p))
-        if name == "sum":
-            value = (
-                kept.astype(jnp.float32)
-                + across(get("tox", p)).astype(jnp.float32)
-                + flip(get("toy", p), 2).astype(jnp.float32)
-            )
-            return value if p == 0 else value.astype(jnp.bfloat16)
-        if name == "back":
-            value = get("sum", p)
-            return value if p == 0 else shift(value, p).astype(jnp.float32)
-
+        if name == "rx":
+            return [to_x + jnp.where(even, zero, done["rdiag", p])]
+        if name == "ry":
+            return [to_y + jnp.where(even, done["rdiag", p], zero)]
+        parts = (kept, done["rx", p], done["ry", p])
+        return [sum(part.astype(jnp.float32) for part in parts).astype(jnp.bfloat16)]
+
+    def run(name, p, values):
+        if name in ("z", "rz"):
+            return [shift(values[0], -p if name == "z" else p)]
+        if name in ("x", "rx"):
+            return [across(values[0])]
+        if name in ("y", "ry"):
+            return [flip(values[0], 2)]
+        if name in ("diag", "rdiag"):
+            return [diagonal(values[0])]
+        order = jnp.stack(
+            [
+                (here // PLANE + plane) % planes * PLANE + ((here % PLANE) ^ flips)
+                for plane in groups[p]
+                for flips in (0, 2)
+            ]
+        )
+        return run_expert(place, values, every_ids[order], top, moe_gain[None], router, weights)
+
+    for phase in phases:
+        outs = [run(*step, operands(*step)) for step in phase]
+        flat = [value for values in outs for value in values]
+        held = list(lax.optimization_barrier((done["z", 0], *flat)))
+        done["z", 0] = held.pop(0)
+        for step, values in zip(phase, outs):
+            values = [held.pop(0) for _ in values]
+            done[step] = values if step[0] == "K" else values[0]
     total = hidden.astype(jnp.float32)
-    for plane in range(planes):
-        total = total + get("back", plane)
+    group = [g for g in range(len(groups)) if 0 in groups[g]][0]
+    total = total + done["K", group][4 * groups[group].index(0)].astype(jnp.float32)
+    total = total + done["rx", 0].astype(jnp.float32) + done["ry", 0].astype(jnp.float32)
+    for plane in range(1, planes):
+        total = total + done["rz", plane].astype(jnp.float32)
     return total.astype(jnp.bfloat16)
 
 
@@ -337,12 +322,26 @@
     return jnp.concatenate([rows, pad], axis=0).T if pad.shape[0] else rows.T
 
 
-def state_kernel(step, rate, x, b, state, running):
+def column_of(row):
+    size = row.shape[1]
+    line = lax.broadcasted_iota(jnp.int32, (size, size), 0)
+    lane = lax.broadcasted_iota(jnp.int32, (size, size), 1)
+    return jnp.sum(jnp.where(line == lane, row, 0.0), axis=1, keepdims=True)
+
+
+def state_kernel(rate, step_hbm, x_hbm, b_hbm, state, running, step, x, b, came):
+    copies = [
+        pltpu.make_async_copy(source, target, came.at[i])
+        for i, (source, target) in enumerate(((step_hbm, step), (x_hbm, x), (b_hbm, b)))
+    ]
+    for copy in copies:
+        copy.start()
     heads, count = step.shape
     groups = b.shape[1] // N
     per_group = heads // groups
     wide = per_group * P_SIZE
-    total = -step[...] * rate[...]
+    copies[0].wait()
+    total = -step[...] * column_of(rate[...])
     lane = lax.broadcasted_iota(jnp.int32, (heads, count), 1)
     hop = 1
     while hop < count:
@@ -350,6 +349,8 @@
         hop *= 2
     running[...] = total
     weight = jnp.exp(total[:, count - 1 :] - total) * step[...]
+    copies[1].wait()
+    copies[2].wait()
     for group in range(groups):
         turned = x[:, group * wide : (group + 1) * wide].astype(jnp.float32).T
         carried = jnp.concatenate(
@@ -365,7 +366,7 @@
         )
 
 
-def inner_kernel(step, running, x, b, c, inner):
+def inner_part(step, running, x, b, c, inner):
     heads, count = step.shape
     groups = b.shape[1] // N
     per_group = heads // groups
@@ -398,9 +399,58 @@
             )
 
 
-def mixer_kernel(
-    place, mine, back, c, inner, running, z, gain, weight, stream, own, theirs, high, low, normed
-):
+def project(place, rows, weight_hbm, weight, came, first, last, give):
+    shares, _, width = weight.shape
+    total = weight_hbm.shape[1] // width
+    copies = []
+    for step in range(first, last):
+        start = pl.multiple_of(lax.rem(place[1] + step, total) * width, width)
+        copies.append(
+            pltpu.make_async_copy(
+                weight_hbm.at[:, pl.ds(start, width)], weight.at[step - first], came.at[step - first]
+            )
+        )
+    yield [copy.start() for copy in copies]
+    for step in range(first, last):
+        copies[step - first].wait()
+        give(
+            step,
+            jnp.dot(rows[...], weight[step - first], preferred_element_type=jnp.float32),
+        )
+    yield
+
+
+def own_kernel(place, normed, weight_hbm, stream, own, weight, came):
+    def give(step, part):
+        own[...] = part + stream[...].astype(jnp.float32)
+
+    for _ in project(place, normed, weight_hbm, weight, came, 0, 1, give):
+        pass
+
+
+def mixer_kernel(place, gain, weight_hbm, *refs):
+    sources, (normed, theirs), refs = refs[:8], refs[8:10], refs[10:]
+    targets, (inner, high, low, weight, came, fetched) = refs[:8], refs[8:]
+    fetches = [
+        pltpu.make_async_copy(source, target, fetched.at[i])
+        for i, (source, target) in enumerate(zip(sources, targets))
+    ]
+    for fetch in fetches:
+        fetch.start()
+    step, running, x, b, c, z, mine, back = targets
+
+    def give(step, part):
+        theirs[step - 1] = part.astype(jnp.bfloat16)
+
+    projection = project(
+        place, normed, weight_hbm, weight, came, 1, theirs.shape[0] + 1, give
+    )
+    next(projection)
+    for fetch in fetches[:5]:
+        fetch.wait()
+    inner_part(step, running, x, b, c, inner)
+    for fetch in fetches[5:]:
+        fetch.wait()
     heads, count = running.shape
     groups = c.shape[1] // N
     per_group = heads // groups
@@ -432,17 +482,7 @@
         gated = (inner[:, where] + scale * carried) * (gate / (1.0 + jnp.exp(-gate)))
         mean = jnp.sum(gated * gated, axis=1, keepdims=True) / wide
         normed[:, where] = (gated * lax.rsqrt(mean + 1e-05) * gain[:, where]).astype(jnp.bfloat16)
-    width = stream.shape[1]
-    shares = theirs.shape[0] + 1
-    for step in range(shares - 1, -1, -1):
-        start = pl.multiple_of(lax.rem(place[1] + step, shares) * width, width)
-        part = jnp.dot(
-            normed[...], weight[:, pl.ds(start, width)], preferred_element_type=jnp.float32
-        )
-        if step:
-            theirs[step - 1] = part.astype(jnp.bfloat16)
-        else:
-            own[...] = part + stream[...].astype(jnp.float32)
+    next(projection)
 
 
 def per_device(
@@ -472,42 +512,62 @@
         2, token_count * top_count // expert_count + token_count * top_count // (4 * expert_count)
     )
     vmem = pl.BlockSpec(memory_space=pltpu.VMEM)
-    wide = jax.ShapeDtypeStruct((token_count, inner_width), jnp.float32)
+    hbm = pl.BlockSpec(memory_space=pltpu.HBM)
     state, running = pl.pallas_call(
         state_kernel,
         out_shape=[
             jax.ShapeDtypeStruct((inner_width, N), jnp.float32),
             jax.ShapeDtypeStruct(step_size.shape, jnp.float32),
         ],
-        in_specs=[vmem] * 4,
+        in_specs=[vmem] + [hbm] * 3,
         out_specs=[vmem] * 2,
+        scratch_shapes=[
+            pltpu.VMEM(step_size.shape, jnp.float32),
+            pltpu.VMEM(ssm_input.shape, jnp.bfloat16),
+            pltpu.VMEM(b_input.shape, jnp.bfloat16),
+            pltpu.SemaphoreType.DMA((3,)),
+        ],
         compiler_params=pltpu.CompilerParams(vmem_limit_bytes=16 * 2**20),
-    )(step_size, decay_rate[:, None], ssm_input, b_input)
+    )(decay_rate[None], step_size, ssm_input, b_input)
     id_rows = jnp.pad(expert_ids.T.astype(jnp.float32), ((0, -expert_ids.shape[1] % 8), (0, 0)))
     mine, back, every_ids = prefix_states(state, running[:, -1], id_rows)
-    inner = pl.pallas_call(
-        inner_kernel,
-        out_shape=wide,
-        in_specs=[vmem] * 5,
-        out_specs=vmem,
-        compiler_params=pltpu.CompilerParams(vmem_limit_bytes=16 * 2**20),
-    )(step_size, running, ssm_input, b_input, c_input)
     place = jnp.stack([lax.axis_index("ctx"), lax.axis_index("exp")]).astype(jnp.int32)
-    hidden_own, theirs = pl.pallas_call(
+    fetched = (step_size, running, ssm_input, b_input, c_input, gate_input, mine, back)
+    normed, theirs = pl.pallas_call(
         mixer_kernel,
         out_shape=[
-            jax.ShapeDtypeStruct(stream.shape, jnp.float32),
+            jax.ShapeDtypeStruct((token_count, inner_width), jnp.bfloat16),
             jax.ShapeDtypeStruct((exp_size - 1, *stream.shape), jnp.bfloat16),
         ],
-        in_specs=[pl.BlockSpec(memory_space=pltpu.SMEM)] + [vmem] * 9,
+        in_specs=[pl.BlockSpec(memory_space=pltpu.SMEM), vmem] + [hbm] * 9,
         out_specs=[vmem] * 2,
-        scratch_shapes=[
+        scratch_shapes=[pltpu.VMEM(array.shape, array.dtype) for array in fetched]
+        + [
+            pltpu.VMEM((token_count, inner_width), jnp.float32),
             pltpu.VMEM((inner_width, N), jnp.bfloat16),
             pltpu.VMEM((inner_width, N), jnp.bfloat16),
-            pltpu.VMEM((token_count, inner_width), jnp.bfloat16),
+            pltpu.VMEM((exp_size - 1, inner_width, slice_width), jnp.bfloat16),
+            pltpu.SemaphoreType.DMA((exp_size - 1,)),
+            pltpu.SemaphoreType.DMA((8,)),
         ],
-        compiler_params=pltpu.CompilerParams(vmem_limit_bytes=24 * 2**20),
-    )(place, mine, back, c_input, inner, running, gate_input, norm_gain[None], out_weight, stream)
+        compiler_params=pltpu.CompilerParams(vmem_limit_bytes=60 * 2**20),
+    )(place, norm_gain[None], out_weight, *fetched)
+    hidden_own = pl.pallas_call(
+        own_kernel,
+        out_shape=jax.ShapeDtypeStruct(stream.shape, jnp.float32),
+        in_specs=[pl.BlockSpec(memory_space=pltpu.SMEM), vmem, hbm, vmem],
+        out_specs=vmem,
+        scratch_shapes=[
+            pltpu.VMEM((1, inner_width, slice_width), jnp.bfloat16),
+            pltpu.SemaphoreType.DMA((1,)),
+        ],
+        compiler_params=pltpu.CompilerParams(vmem_limit_bytes=60 * 2**20),
+        cost_estimate=pl.CostEstimate(
+            flops=2 * token_count * inner_width * slice_width,
+            bytes_accessed=2 * inner_width * slice_width,
+            transcendentals=0,
+        ),
+    )(place, normed, out_weight, stream)
     for step in range(1, exp_size):
         ring = [(i, (i + step) % exp_size) for i in range(exp_size)]
         sent = lax.ppermute(theirs[step - 1], "exp", ring)

time: 209 us -> 198 us (0.947)
  waiting for transfers between devices: 86.3 us -> 53.1 us
  Pallas kernels: 44.3 us -> 58.2 us
  other arithmetic: 5.06 us -> 10.4 us
  starting transfers between devices: 34.5 us -> 38.7 us
    ppermute x8, waiting for transfers between devices: 19.7 us -> 4.91 us  [diagonal(): return lax.ppermute(value, ('ctx', 'exp'), pairs)]
    ppermute x8, waiting for transfers between devices: 10.8 us -> 2.6 us  [across(): return lax.ppermute(value, 'exp', [(0, 1), (1, 0)])]
    pallas_call x2 -> x4, Pallas kernels: 36.6 us -> 44.1 us  [run_expert(): pl.pallas_call(functools.partial(expert_kernel, planes, top), out_shape=[...]
    pallas_call x2, Pallas kernels: 4.43 us -> 10.7 us  [the longest x1 5.86 us: per_device(): pl.pallas_call(mixer_kernel, out_shape=[jax.ShapeDtypeStruct((token_count...]
    ppermute x19, waiting for transfers between devices: 35.6 us -> 30.1 us  [move(): lax.ppermute(value, 'ctx', [(i, partner(i)) for i in range(lax.axis_size(...]
    ppermute x1, waiting for transfers between devices: 6.85 us -> 2.18 us  [per_device(): sent = lax.ppermute(theirs[step - 1], 'exp', ring)]
    unnamed x31 -> x65, local copies, waits for them, and re-layouts: 10 us -> 5.34 us
    ppermute x19, starting transfers between devices: 11.8 us -> 16.2 us  [move(): lax.ppermute(value, 'ctx', [(i, partner(i)) for i in range(lax.axis_size(...]
  transfers between devices with their start and end apart: 37 -> 37, of which waited for: 20 -> 19; matrix products, arithmetic and copies ran while one was open for 3% -> 7% of each run, Pallas kernels for 11% -> 28%
where the time goes in v2:
time: 198 us; the launch traced here: 197 us
  Pallas kernels  58.2 us (29%)
  waiting for transfers between devices  53.1 us (27%)
  starting transfers between devices  38.7 us (20%)
  blocking collectives  24.8 us (13%)
  local copies, waits for them, and re-layouts  11.4 us (6%)
  other arithmetic  10.4 us (5%)
    pallas_call x4, Pallas kernels, run_expert(): pl.pallas_call(functools.partial(expert_kernel, planes, top), out_shape=[...  44.1 us
    ppermute x19, waiting for transfers between devices, move(): lax.ppermute(value, 'ctx', [(i, partner(i)) for i in range(lax.axis_size(...  30.1 us
    all_to_all x1, blocking collectives, exchange(): lax.all_to_all(array, 'ctx', split_axis=0, concat_axis=0, axis_index_grou...  24.8 us
    ppermute x19, starting transfers between devices, move(): lax.ppermute(value, 'ctx', [(i, partner(i)) for i in range(lax.axis_size(...  16.2 us
    all_to_all x1, waiting for transfers between devices, exchange(): lax.all_to_all(array, 'ctx', split_axis=0, concat_axis=0, axis_index_grou...  13.4 us
    ppermute x8, starting transfers between devices, diagonal(): return lax.ppermute(value, ('ctx', 'exp'), pairs)  10.1 us
    ppermute x8, starting transfers between devices, across(): return lax.ppermute(value, 'exp', [(0, 1), (1, 0)])  7.34 us
    pallas_call x1, Pallas kernels, per_device(): pl.pallas_call(mixer_kernel, out_shape=[jax.ShapeDtypeStruct((token_count...  5.86 us
  transfers between devices with their start and end apart: 37, of which 19 were waited for; matrix products, arithmetic and copies ran while one was open for 7% of the time, Pallas kernels for 28%

profile of v2, /device:TPU:0, one launch (start us, length us, event | category | flops | bytes accessed | tf_op | source)
XLA Modules:
  0.0 197.0 jit_solution(12225838591395287805)
XLA Ops:
  9.0 24.8 %all_to_all.10.pairs = f32[8,152,128]{2,1,0:T(8,128)} all-to-all(f32[8,152,128]{2,1,0:T(8,128)S(1)} %fusion), channel_id=1, replica_groups={{0,4,8,12,16,20,24,28},{2,6,10,14,18,22,26,30},{1,5,9,13,17,21,25,29},{..., dimensions={0} | all-to-all | bytes 1245184 | tf_op jit(solution)/shard_map/all_to_all | solution.py:73
  33.7 2.1 %shard_map.146 = f32[8,128,128]{2,1,0:T(8,128)} custom-call(f32[8,152,128]{2,1,0:T(8,128)} %all_to_all.10.pairs), custom_call_target="tpu_custom_call" | custom-call | tf_op jit(solution)/shard_map/pallas_call | solution.py:78
  35.8 3.5 %all-to-all-start.1 = ((f32[8,128,128]{2,1,0:T(8,128)}), f32[8,128,128]{2,1,0:T(8,128)S(1)}, u32[]{:S(2)}, u32[]{:S(2)}) async-start(f32[8,128,128]{2,1,0:T(8,128)} %shard_map.146), calls=%async_computation.1 | async-start | bytes 1048576 | tf_op jit(solution)/shard_map/all_to_all | solution.py:73
  40.0 13.4 %all-to-all-done.1 = f32[8,128,128]{2,1,0:T(8,128)S(1)} async-done(((f32[8,128,128]{2,1,0:T(8,128)}), f32[8,128,128]{2,1,0:T(8,128)S(1)}, u32[]{:S(2)}, u32[]{:S(2)}) %all-to-all-start.1) | async-done | bytes 524320 | tf_op jit(solution)/shard_map/all_to_all | solution.py:73
  53.3 2.3 %bitcast_select_fusion = (f32[1024,128]{1,0:T(8,128)}, f32[1024,128]{1,0:T(8,128)}) fusion(f32[8,128,128]{2,1,0:T(8,128)S(1)} %all-to-all-done.1, f32[1024,128]{1,0:T(8,128)} %get-tuple-element.144, f32[1024]{0:T(1024)S(1)} %get-tuple-element.147, pred[]{:T(512)S(6)} %eq.25), kind=kLoop, calls=%fused_computation.10 | loop fusion | flops 524288 | bytes 2101249 | tf_op jit(solution)/shard_map/jit(_where)/select_n | solution.py:49
  58.5 5.9 %shard_map.147 = (bf16[128,2048]{1,0:T(8,128)(2,1)}, bf16[1,128,1024]{2,1,0:T(8,128)(2,1)}) custom-call(s32[2]{0:T(128)} %pad_add_fusion.place, f32[1,2048]{1,0:T(1,128)} %bitcast.76, bf16[2048,2048]{1,0:T(8,128)(2,1)} %weight_hbm.3, f32[32,128]{1,0:T(8,128)} %refs_0_.1, f32[32,128]{1,0:T(8,128)} %copy-done.3, bf16[128,2048]{1,0:T(8,128)(2,1)} %refs_2_.1, ...), custom_call_target="tpu_custom_call" | custom-call | tf_op jit(solution)/shard_map/pallas_call | solution.py:536
  66.0 4.9 %shard_map.148 = f32[128,1024]{1,0:T(8,128)} custom-call(s32[2]{0:T(128)} %pad_add_fusion.place, bf16[128,2048]{1,0:T(8,128)(2,1)} %get-tuple-element.75.normed, bf16[2048,2048]{1,0:T(8,128)(2,1)} %weight_hbm.3, bf16[128,1024]{1,0:T(8,128)(2,1)} %stream.1), custom_call_target="tpu_custom_call" | custom-call | flops 536870912 | bytes 4194304 | tf_op jit(solution)/shard_map/pallas_call | solution.py:555
  70.8 2.2 %collective-permute-done.2 = bf16[128,1024]{1,0:T(8,128)(2,1)S(1)} collective-permute-done((bf16[128,1024]{1,0:T(8,128)(2,1)}, bf16[128,1024]{1,0:T(8,128)(2,1)S(1)}, u32[]{:S(2)}, u32[]{:S(2)}) %collective-permute-start.2) | collective-permute-done | bytes 262176 | tf_op jit(solution)/shard_map/ppermute | solution.py:573
  77.9 3.8 %collective-permute-done.4.refs_2_ = bf16[128,1024]{1,0:T(8,128)(2,1)S(1)} collective-permute-done((bf16[128,1024]{1,0:T(8,128)(2,1)S(1)}, bf16[128,1024]{1,0:T(8,128)(2,1)S(1)}, u32[]{:S(2)}, u32[]{:S(2)}) %collective-permute-start.4) | collective-permute-done | bytes 262176 | tf_op jit(solution)/shard_map/ppermute | solution.py:16
  94.6 11.0 %shard_map.149 = (bf16[128,1024]{1,0:T(8,128)(2,1)}, bf16[128,1024]{1,0:T(8,128)(2,1)}, bf16[128,1024]{1,0:T(8,128)(2,1)}, bf16[128,1024]{1,0:T(8,128)(2,1)}) custom-call(s32[3]{0:T(128)} %pad_add_fusion.1.place, bf16[128,1024]{1,0:T(8,128)(2,1)} %copy-done.6, bf16[128,1024]{1,0:T(8,128)(2,1)} %collective-permute-done.3.refs_1_, ...), custom_call_target="tpu_custom_call" | custom-call | flops 4429185024 | bytes 19398656 | tf_op jit(solution)/shard_map/pallas_call | solution.py:186
  108.1 1.6 collective-permute-start.13
  109.7 2.4 %collective-permute-start.16 = (bf16[128,1024]{1,0:T(8,128)(2,1)}, bf16[128,1024]{1,0:T(8,128)(2,1)S(1)}, u32[]{:S(2)}, u32[]{:S(2)}) collective-permute-start(bf16[128,1024]{1,0:T(8,128)(2,1)} %copy-done.6), channel_id=1, source_target_pairs={{0,8},{2,10},{4,12},{6,14},{8,16},{10,18},{12,20},{14,22},{16,24},... | collective-permute-start | bytes 786440 | tf_op jit(solution)/shard_map/ppermute | solution.py:16
  118.2 1.8 collective-permute-start.18
  122.1 11.0 %shard_map.150 = (bf16[128,1024]{1,0:T(8,128)(2,1)}, bf16[128,1024]{1,0:T(8,128)(2,1)}, bf16[128,1024]{1,0:T(8,128)(2,1)}, bf16[128,1024]{1,0:T(8,128)(2,1)}) custom-call(s32[3]{0:T(128)} %pad_add_fusion.1.place, bf16[128,1024]{1,0:T(8,128)(2,1)} %collective-permute-done.6.refs_0_, bf16[128,1024]{1,0:T(8,128)(2,1)} %copy-done.14, ...), custom_call_target="tpu_custom_call" | custom-call | flops 4429185024 | bytes 19398656 | tf_op jit(solution)/shard_map/pallas_call | solution.py:186
  135.8 1.7 collective-permute-start.24
  137.6 11.0 %shard_map.151 = (bf16[128,1024]{1,0:T(8,128)(2,1)}, bf16[128,1024]{1,0:T(8,128)(2,1)}, bf16[128,1024]{1,0:T(8,128)(2,1)}, bf16[128,1024]{1,0:T(8,128)(2,1)}) custom-call(s32[3]{0:T(128)} %pad_add_fusion.1.place, bf16[128,1024]{1,0:T(8,128)(2,1)} %copy-done.17, bf16[128,1024]{1,0:T(8,128)(2,1)} %copy-done.12, bf16[128,1024]{1,0:T(8,128)(2,1)} %copy-done.11, ...), custom_call_target="tpu_custom_call" | custom-call | flops 4429185024 | bytes 19398656 | tf_op jit(solution)/shard_map/pallas_call | solution.py:186
  151.4 11.0 %shard_map.152 = (bf16[128,1024]{1,0:T(8,128)(2,1)}, bf16[128,1024]{1,0:T(8,128)(2,1)}, bf16[128,1024]{1,0:T(8,128)(2,1)}, bf16[128,1024]{1,0:T(8,128)(2,1)}) custom-call(s32[3]{0:T(128)} %pad_add_fusion.1.place, bf16[128,1024]{1,0:T(8,128)(2,1)} %copy-done.16, bf16[128,1024]{1,0:T(8,128)(2,1)} %copy-done.10, bf16[128,1024]{1,0:T(8,128)(2,1)} %copy-done.9, ...), custom_call_target="tpu_custom_call" | custom-call | flops 4429185024 | bytes 19398656 | tf_op jit(solution)/shard_map/pallas_call | solution.py:186
  164.5 1.7 collective-permute-start.30
  166.4 3.3 %collective-permute-done.29 = bf16[128,1024]{1,0:T(8,128)(2,1)S(1)} collective-permute-done((bf16[128,1024]{1,0:T(8,128)(2,1)S(1)}, bf16[128,1024]{1,0:T(8,128)(2,1)S(1)}, u32[]{:S(2)}, u32[]{:S(2)}) %collective-permute-start.29) | collective-permute-done | bytes 262176 | tf_op jit(solution)/shard_map/ppermute | solution.py:16
  170.5 3.2 %collective-permute-done.30 = bf16[128,1024]{1,0:T(8,128)(2,1)S(1)} collective-permute-done((bf16[128,1024]{1,0:T(8,128)(2,1)}, bf16[128,1024]{1,0:T(8,128)(2,1)S(1)}, u32[]{:S(2)}, u32[]{:S(2)}) %collective-permute-start.30) | collective-permute-done | bytes 262176 | tf_op jit(solution)/shard_map/ppermute | solution.py:227
  177.9 4.2 %collective-permute-done.33 = bf16[128,1024]{1,0:T(8,128)(2,1)S(1)} collective-permute-done((bf16[128,1024]{1,0:T(8,128)(2,1)S(1)}, bf16[128,1024]{1,0:T(8,128)(2,1)S(1)}, u32[]{:S(2)}, u32[]{:S(2)}) %collective-permute-start.33) | collective-permute-done | bytes 262176 | tf_op jit(solution)/shard_map/ppermute | solution.py:16
  182.6 6.8 %collective-permute-done.34 = bf16[128,1024]{1,0:T(8,128)(2,1)S(1)} collective-permute-done((bf16[128,1024]{1,0:T(8,128)(2,1)S(1)}, bf16[128,1024]{1,0:T(8,128)(2,1)S(1)}, u32[]{:S(2)}, u32[]{:S(2)}) %collective-permute-start.34) | collective-permute-done | bytes 262176 | tf_op jit(solution)/shard_map/ppermute | solution.py:16
  189.6 1.6 collective-permute-start.35
  191.2 4.8 %collective-permute-done.35 = bf16[128,1024]{1,0:T(8,128)(2,1)S(1)} collective-permute-done((bf16[128,1024]{1,0:T(8,128)(2,1)S(1)}, bf16[128,1024]{1,0:T(8,128)(2,1)S(1)}, u32[]{:S(2)}, u32[]{:S(2)}) %collective-permute-start.35) | collective-permute-done | bytes 262176 | tf_op jit(solution)/shard_map/ppermute | solution.py:16
  (172 shorter events, 56.4 us)
Async XLA Ops:
  35.8 17.5 %all-to-all-start.1 = ((f32[8,128,128]{2,1,0:T(8,128)}), f32[8,128,128]{2,1,0:T(8,128)S(1)}, u32[]{:S(2)}, u32[]{:S(2)}) async-start(f32[8,128,128]{2,1,0:T(8,128)} %shard_map.146), calls=%async_computation.1 | async-start | bytes 1048576 | tf_op jit(solution)/shard_map/all_to_all | solution.py:73
  39.3 55.0 %collective-permute-start.7 = (bf16[704,2048]{1,0:T(8,128)(2,1)S(1)}, bf16[704,2048]{1,0:T(8,128)(2,1)}, u32[]{:S(2)}, u32[]{:S(2)}) collective-permute-start(bf16[704,2048]{1,0:T(8,128)(2,1)S(1)} %bitcast.55), channel_id=1, source_target_pairs={{0,2},{2,0},{4,6},{6,4},{8,10},{10,8},{12,14},{14,12},{16,18},{18,... | collective-permute-start | bytes 8650760 | tf_op jit(solution)/shard_map/ppermute | solution.py:16
  39.4 55.2 %collective-permute-start.8 = (bf16[704,2048]{1,0:T(8,128)(2,1)}, bf16[704,2048]{1,0:T(8,128)(2,1)}, u32[]{:S(2)}, u32[]{:S(2)}) collective-permute-start(bf16[704,2048]{1,0:T(8,128)(2,1)} %bitcast.56), channel_id=1, source_target_pairs={{0,2},{2,0},{4,6},{6,4},{8,10},{10,8},{12,14},{14,12},{16,18},{18,... | collective-permute-start | bytes 8650760 | tf_op jit(solution)/shard_map/ppermute | solution.py:16
  39.9 54.7 %collective-permute-start.9 = (bf16[704,2048]{1,0:T(8,128)(2,1)}, bf16[704,2048]{1,0:T(8,128)(2,1)}, u32[]{:S(2)}, u32[]{:S(2)}) collective-permute-start(bf16[704,2048]{1,0:T(8,128)(2,1)} %bitcast.61), channel_id=1, source_target_pairs={{0,2},{2,0},{4,6},{6,4},{8,10},{10,8},{12,14},{14,12},{16,18},{18,... | collective-permute-start | bytes 8650760 | tf_op jit(solution)/shard_map/ppermute | solution.py:16
  64.4 8.6 %collective-permute-start.2 = (bf16[128,1024]{1,0:T(8,128)(2,1)}, bf16[128,1024]{1,0:T(8,128)(2,1)S(1)}, u32[]{:S(2)}, u32[]{:S(2)}) collective-permute-start(bf16[128,1024]{1,0:T(8,128)(2,1)} %bitcast.77), channel_id=1, source_target_pairs={{0,1},{1,0},{2,3},{3,2},{4,5},{5,4},{6,7},{7,6},{8,9},{9,8},{10,11... | collective-permute-start | bytes 786440 | tf_op jit(solution)/shard_map/ppermute | solution.py:573
  91.7 15.6 %collective-permute-start.11 = (bf16[128,1024]{1,0:T(8,128)(2,1)}, bf16[128,1024]{1,0:T(8,128)(2,1)S(1)}, u32[]{:S(2)}, u32[]{:S(2)}) collective-permute-start(bf16[128,1024]{1,0:T(8,128)(2,1)} %collective-permute-done.6.refs_0_), channel_id=1, source_target_pairs={{0,4},{2,6},{4,0},{6,2},{8,12},{10,14},{12,8},{14,10},{16,20},{18,... | collective-permute-start | bytes 786440 | tf_op jit(solution)/shard_map/ppermute | solution.py:16
  92.8 14.4 %collective-permute-start.10 = (bf16[128,1024]{1,0:T(8,128)(2,1)}, bf16[128,1024]{1,0:T(8,128)(2,1)S(1)}, u32[]{:S(2)}, u32[]{:S(2)}) collective-permute-start(bf16[128,1024]{1,0:T(8,128)(2,1)} %collective-permute-done.6.refs_0_), channel_id=1, source_target_pairs={{0,1},{1,0},{2,3},{3,2},{4,5},{5,4},{6,7},{7,6},{8,9},{9,8},{10,11... | collective-permute-start | bytes 786440 | tf_op jit(solution)/shard_map/ppermute | solution.py:219
  94.3 12.9 %collective-permute-start.12 = (bf16[128,1024]{1,0:T(8,128)(2,1)S(1)}, bf16[128,1024]{1,0:T(8,128)(2,1)S(1)}, u32[]{:S(2)}, u32[]{:S(2)}) collective-permute-start(bf16[128,1024]{1,0:T(8,128)(2,1)S(1)} %add_convert_fusion.4.refs_0_), channel_id=1, source_target_pairs={{0,16},{2,18},{4,20},{6,22},{8,24},{10,26},{12,28},{14,30},{16,0},... | collective-permute-start | bytes 786440 | tf_op jit(solution)/shard_map/ppermute | solution.py:16
  107.2 10.9 %collective-permute-start.15 = (bf16[128,1024]{1,0:T(8,128)(2,1)S(1)}, bf16[128,1024]{1,0:T(8,128)(2,1)S(1)}, u32[]{:S(2)}, u32[]{:S(2)}) collective-permute-start(bf16[128,1024]{1,0:T(8,128)(2,1)S(1)} %collective-permute-done.12.refs_0_), channel_id=1, source_target_pairs={{0,4},{2,6},{4,0},{6,2},{8,12},{10,14},{12,8},{14,10},{16,20},{18,... | collective-permute-start | bytes 786440 | tf_op jit(solution)/shard_map/ppermute | solution.py:16
  107.6 10.6 %collective-permute-start.14 = (bf16[128,1024]{1,0:T(8,128)(2,1)S(1)}, bf16[128,1024]{1,0:T(8,128)(2,1)S(1)}, u32[]{:S(2)}, u32[]{:S(2)}) collective-permute-start(bf16[128,1024]{1,0:T(8,128)(2,1)S(1)} %collective-permute-done.12.refs_0_), channel_id=1, source_target_pairs={{0,1},{1,0},{2,3},{3,2},{4,5},{5,4},{6,7},{7,6},{8,9},{9,8},{10,11... | collective-permute-start | bytes 786440 | tf_op jit(solution)/shard_map/ppermute | solution.py:219
  108.1 9.4 %collective-permute-start.13 = (bf16[128,1024]{1,0:T(8,128)(2,1)S(1)}, bf16[128,1024]{1,0:T(8,128)(2,1)S(1)}, u32[]{:S(2)}, u32[]{:S(2)}) collective-permute-start(bf16[128,1024]{1,0:T(8,128)(2,1)S(1)} %broadcast_select_fusion.2), channel_id=1, source_target_pairs={{0,1},{1,0},{2,6},{3,7},{4,5},{5,4},{6,2},{7,3},{8,9},{9,8},{10,14... | collective-permute-start | bytes 786440 | tf_op jit(solution)/shard_map/ppermute | solution.py:227
  115.6 17.5 %collective-permute-start.20 = (bf16[128,1024]{1,0:T(8,128)(2,1)}, bf16[128,1024]{1,0:T(8,128)(2,1)S(1)}, u32[]{:S(2)}, u32[]{:S(2)}) collective-permute-start(bf16[128,1024]{1,0:T(8,128)(2,1)} %get-tuple-element.100), channel_id=1, source_target_pairs={{0,1},{1,0},{2,6},{3,7},{4,5},{5,4},{6,2},{7,3},{8,9},{9,8},{10,14... | collective-permute-start | bytes 786440 | tf_op jit(solution)/shard_map/ppermute | solution.py:227
  118.2 15.0 %collective-permute-start.18 = (bf16[128,1024]{1,0:T(8,128)(2,1)S(1)}, bf16[128,1024]{1,0:T(8,128)(2,1)S(1)}, u32[]{:S(2)}, u32[]{:S(2)}) collective-permute-start(bf16[128,1024]{1,0:T(8,128)(2,1)S(1)} %collective-permute-done.16.refs_0_), channel_id=1, source_target_pairs={{0,4},{2,6},{4,0},{6,2},{8,12},{10,14},{12,8},{14,10},{16,20},{18,... | collective-permute-start | bytes 786440 | tf_op jit(solution)/shard_map/ppermute | solution.py:16
  119.9 13.3 %collective-permute-start.17 = (bf16[128,1024]{1,0:T(8,128)(2,1)S(1)}, bf16[128,1024]{1,0:T(8,128)(2,1)S(1)}, u32[]{:S(2)}, u32[]{:S(2)}) collective-permute-start(bf16[128,1024]{1,0:T(8,128)(2,1)S(1)} %collective-permute-done.16.refs_0_), channel_id=1, source_target_pairs={{0,1},{1,0},{2,3},{3,2},{4,5},{5,4},{6,7},{7,6},{8,9},{9,8},{10,11... | collective-permute-start | bytes 786440 | tf_op jit(solution)/shard_map/ppermute | solution.py:219
  120.6 12.6 %collective-permute-start.19 = (bf16[128,1024]{1,0:T(8,128)(2,1)S(1)}, bf16[128,1024]{1,0:T(8,128)(2,1)S(1)}, u32[]{:S(2)}, u32[]{:S(2)}) collective-permute-start(bf16[128,1024]{1,0:T(8,128)(2,1)S(1)} %broadcast_select_fusion.1), channel_id=1, source_target_pairs={{0,1},{1,0},{2,6},{3,7},{4,5},{5,4},{6,2},{7,3},{8,9},{9,8},{10,14... | collective-permute-start | bytes 786440 | tf_op jit(solution)/shard_map/ppermute | solution.py:227
  133.3 15.3 %collective-permute-start.21 = (bf16[128,1024]{1,0:T(8,128)(2,1)S(1)}, bf16[128,1024]{1,0:T(8,128)(2,1)S(1)}, u32[]{:S(2)}, u32[]{:S(2)}) collective-permute-start(bf16[128,1024]{1,0:T(8,128)(2,1)S(1)} %broadcast_select_fusion), channel_id=1, source_target_pairs={{0,1},{1,0},{2,6},{3,7},{4,5},{5,4},{6,2},{7,3},{8,9},{9,8},{10,14... | collective-permute-start | bytes 786440 | tf_op jit(solution)/shard_map/ppermute | solution.py:227
  134.0 14.6 %collective-permute-start.23 = (bf16[128,1024]{1,0:T(8,128)(2,1)S(1)}, bf16[128,1024]{1,0:T(8,128)(2,1)S(1)}, u32[]{:S(2)}, u32[]{:S(2)}) collective-permute-start(bf16[128,1024]{1,0:T(8,128)(2,1)S(1)} %get-tuple-element.158), channel_id=1, source_target_pairs={{0,4},{2,6},{4,0},{6,2},{8,12},{10,14},{12,8},{14,10},{16,20},{18,... | collective-permute-start | bytes 786440 | tf_op jit(solution)/shard_map/ppermute | solution.py:16
  135.6 13.1 %collective-permute-start.22 = (bf16[128,1024]{1,0:T(8,128)(2,1)S(1)}, bf16[128,1024]{1,0:T(8,128)(2,1)S(1)}, u32[]{:S(2)}, u32[]{:S(2)}) collective-permute-start(bf16[128,1024]{1,0:T(8,128)(2,1)S(1)} %get-tuple-element.159), channel_id=1, source_target_pairs={{0,1},{1,0},{2,3},{3,2},{4,5},{5,4},{6,7},{7,6},{8,9},{9,8},{10,11... | collective-permute-start | bytes 786440 | tf_op jit(solution)/shard_map/ppermute | solution.py:219
  135.8 12.8 %collective-permute-start.24 = (bf16[128,1024]{1,0:T(8,128)(2,1)}, bf16[128,1024]{1,0:T(8,128)(2,1)S(1)}, u32[]{:S(2)}, u32[]{:S(2)}) collective-permute-start(bf16[128,1024]{1,0:T(8,128)(2,1)} %get-tuple-element.111), channel_id=1, source_target_pairs={{0,1},{1,0},{2,6},{3,7},{4,5},{5,4},{6,2},{7,3},{8,9},{9,8},{10,14... | collective-permute-start | bytes 786440 | tf_op jit(solution)/shard_map/ppermute | solution.py:227
  148.7 13.7 %collective-permute-start.26 = (bf16[128,1024]{1,0:T(8,128)(2,1)S(1)}, bf16[128,1024]{1,0:T(8,128)(2,1)S(1)}, u32[]{:S(2)}, u32[]{:S(2)}) collective-permute-start(bf16[128,1024]{1,0:T(8,128)(2,1)S(1)} %get-tuple-element.156), channel_id=1, source_target_pairs={{0,4},{2,6},{4,0},{6,2},{8,12},{10,14},{12,8},{14,10},{16,20},{18,... | collective-permute-start | bytes 786440 | tf_op jit(solution)/shard_map/ppermute | solution.py:16
  149.4 13.1 %collective-permute-start.25 = (bf16[128,1024]{1,0:T(8,128)(2,1)S(1)}, bf16[128,1024]{1,0:T(8,128)(2,1)S(1)}, u32[]{:S(2)}, u32[]{:S(2)}) collective-permute-start(bf16[128,1024]{1,0:T(8,128)(2,1)S(1)} %get-tuple-element.157), channel_id=1, source_target_pairs={{0,1},{1,0},{2,3},{3,2},{4,5},{5,4},{6,7},{7,6},{8,9},{9,8},{10,11... | collective-permute-start | bytes 786440 | tf_op jit(solution)/shard_map/ppermute | solution.py:219
  150.8 11.7 %collective-permute-start.27 = (bf16[128,1024]{1,0:T(8,128)(2,1)}, bf16[128,1024]{1,0:T(8,128)(2,1)S(1)}, u32[]{:S(2)}, u32[]{:S(2)}) collective-permute-start(bf16[128,1024]{1,0:T(8,128)(2,1)} %get-tuple-element.123), channel_id=1, source_target_pairs={{0,1},{1,0},{2,6},{3,7},{4,5},{5,4},{6,2},{7,3},{8,9},{9,8},{10,14... | collective-permute-start | bytes 786440 | tf_op jit(solution)/shard_map/ppermute | solution.py:227
  164.5 9.3 %collective-permute-start.30 = (bf16[128,1024]{1,0:T(8,128)(2,1)}, bf16[128,1024]{1,0:T(8,128)(2,1)S(1)}, u32[]{:S(2)}, u32[]{:S(2)}) collective-permute-start(bf16[128,1024]{1,0:T(8,128)(2,1)} %get-tuple-element.126), channel_id=1, source_target_pairs={{0,1},{1,0},{2,6},{3,7},{4,5},{5,4},{6,2},{7,3},{8,9},{9,8},{10,14... | collective-permute-start | bytes 786440 | tf_op jit(solution)/shard_map/ppermute | solution.py:227
  177.8 11.7 %collective-permute-start.34 = (bf16[128,1024]{1,0:T(8,128)(2,1)S(1)}, bf16[128,1024]{1,0:T(8,128)(2,1)S(1)}, u32[]{:S(2)}, u32[]{:S(2)}) collective-permute-start(bf16[128,1024]{1,0:T(8,128)(2,1)S(1)} %add_convert_fusion.2), channel_id=1, source_target_pairs={{0,16},{2,18},{4,20},{6,22},{8,24},{10,26},{12,28},{14,30},{16,0},... | collective-permute-start | bytes 786440 | tf_op jit(solution)/shard_map/ppermute | solution.py:16
  (45 other events, 494.2 us)

commit v3 on v2

--- a/solution.py
+++ b/solution.py
@@ -33,7 +33,7 @@
         entering = decay * entering + pairs[pair, :share]
 
 
-def prefix_states(state, log_total, extra):
+def prefix_states(state, log_total, extra, beside):
     size = lax.axis_size("ctx")
     odd = lax.axis_index("ctx") % 2 == 1
     rows, width = state.shape
@@ -79,10 +79,12 @@
         chain_kernel, out_shape=jax.ShapeDtypeStruct((size // 2, share, width), jnp.float32)
     )(pairs)
     into_first = exchange(found).reshape(half, width)
+    into_first, beside = lax.optimization_barrier((into_first, beside))
     into_second = jnp.exp(first_log)[:, None] * into_first + first
-    mine, other = pick(odd, into_first, into_second), pick(odd, into_second, into_first)
-    back = move(other, lambda i: i ^ 1)
-    return mine, back, pairs[:, share + 8 :].reshape(size, extra_rows, width)
+    back = move(pick(odd, into_second, into_first), lambda i: i ^ 1)
+    into_first, first, first_log = lax.optimization_barrier((into_first, first, first_log))
+    mine = pick(odd, into_first, jnp.exp(first_log)[:, None] * into_first + first)
+    return mine, back, beside, pairs[:, share + 8 :].reshape(size, extra_rows, width)
 
 
 def expert_kernel(planes, top, place, *refs):
@@ -206,10 +208,10 @@
     )(place, *pieces, ids, moe_gain, router, *weights)
 
 
-def dense_experts(hidden, every_ids, top, moe_gain, router, weights):
+def dense_experts(place, hidden, every_ids, top, moe_gain, router, weights):
     size = lax.axis_size("ctx")
     planes = size // PLANE
-    here, side = lax.axis_index("ctx"), lax.axis_index("exp")
+    here = lax.axis_index("ctx")
     even = here % 2 == 0
 
     def flip(value, bit):
@@ -243,7 +245,6 @@
         [("rx", 3), ("ry", 3), ("rz", 2)],
         [("rz", 3)],
     ]
-    place = jnp.stack([here, side, here ^ 1]).astype(jnp.int32)
     done = {("z", 0): hidden}
 
     def operands(name, p):
@@ -366,7 +367,7 @@
         )
 
 
-def inner_part(step, running, x, b, c, inner):
+def inner_kernel(step, running, x, b, c, inner):
     heads, count = step.shape
     groups = b.shape[1] // N
     per_group = heads // groups
@@ -428,16 +429,16 @@
         pass
 
 
-def mixer_kernel(place, gain, weight_hbm, *refs):
-    sources, (normed, theirs), refs = refs[:8], refs[8:10], refs[10:]
-    targets, (inner, high, low, weight, came, fetched) = refs[:8], refs[8:]
+def mixer_kernel(place, weight_hbm, *refs):
+    sources, (normed, theirs), refs = refs[:7], refs[7:9], refs[9:]
+    targets, (high, low, weight, came, fetched) = refs[:7], refs[7:]
     fetches = [
         pltpu.make_async_copy(source, target, fetched.at[i])
         for i, (source, target) in enumerate(zip(sources, targets))
     ]
     for fetch in fetches:
         fetch.start()
-    step, running, x, b, c, z, mine, back = targets
+    inner, running, c, z, mine, back, gain = targets
 
     def give(step, part):
         theirs[step - 1] = part.astype(jnp.bfloat16)
@@ -446,10 +447,7 @@
         place, normed, weight_hbm, weight, came, 1, theirs.shape[0] + 1, give
     )
     next(projection)
-    for fetch in fetches[:5]:
-        fetch.wait()
-    inner_part(step, running, x, b, c, inner)
-    for fetch in fetches[5:]:
+    for fetch in fetches:
         fetch.wait()
     heads, count = running.shape
     groups = c.shape[1] // N
@@ -530,28 +528,48 @@
         compiler_params=pltpu.CompilerParams(vmem_limit_bytes=16 * 2**20),
     )(decay_rate[None], step_size, ssm_input, b_input)
     id_rows = jnp.pad(expert_ids.T.astype(jnp.float32), ((0, -expert_ids.shape[1] % 8), (0, 0)))
-    mine, back, every_ids = prefix_states(state, running[:, -1], id_rows)
-    place = jnp.stack([lax.axis_index("ctx"), lax.axis_index("exp")]).astype(jnp.int32)
-    fetched = (step_size, running, ssm_input, b_input, c_input, gate_input, mine, back)
+    inner = pl.pallas_call(
+        inner_kernel,
+        out_shape=jax.ShapeDtypeStruct((token_count, inner_width), jnp.float32),
+        in_specs=[vmem] * 5,
+        out_specs=vmem,
+        compiler_params=pltpu.CompilerParams(vmem_limit_bytes=16 * 2**20),
+        cost_estimate=pl.CostEstimate(
+            flops=4 * inner_width * token_count * token_count,
+            bytes_accessed=8 * inner_width * token_count,
+            transcendentals=head_count * token_count * token_count,
+        ),
+    )(step_size, running, ssm_input, b_input, c_input)
+    mine, back, inner, every_ids = prefix_states(state, running[:, -1], id_rows, inner)
+    here = lax.axis_index("ctx")
+    place = jnp.stack([here, lax.axis_index("exp"), here ^ 1]).astype(jnp.int32)
+    fetched = (
+        inner,
+        running,
+        c_input,
+        gate_input,
+        mine,
+        back,
+        norm_gain[None],
+    )
     normed, theirs = pl.pallas_call(
         mixer_kernel,
         out_shape=[
             jax.ShapeDtypeStruct((token_count, inner_width), jnp.bfloat16),
             jax.ShapeDtypeStruct((exp_size - 1, *stream.shape), jnp.bfloat16),
         ],
-        in_specs=[pl.BlockSpec(memory_space=pltpu.SMEM), vmem] + [hbm] * 9,
+        in_specs=[pl.BlockSpec(memory_space=pltpu.SMEM)] + [hbm] * 8,
         out_specs=[vmem] * 2,
         scratch_shapes=[pltpu.VMEM(array.shape, array.dtype) for array in fetched]
         + [
-            pltpu.VMEM((token_count, inner_width), jnp.float32),
             pltpu.VMEM((inner_width, N), jnp.bfloat16),
             pltpu.VMEM((inner_width, N), jnp.bfloat16),
             pltpu.VMEM((exp_size - 1, inner_width, slice_width), jnp.bfloat16),
             pltpu.SemaphoreType.DMA((exp_size - 1,)),
-            pltpu.SemaphoreType.DMA((8,)),
+            pltpu.SemaphoreType.DMA((7,)),
         ],
         compiler_params=pltpu.CompilerParams(vmem_limit_bytes=60 * 2**20),
-    )(place, norm_gain[None], out_weight, *fetched)
+    )(place, out_weight, *fetched)
     hidden_own = pl.pallas_call(
         own_kernel,
         out_shape=jax.ShapeDtypeStruct(stream.shape, jnp.float32),
@@ -576,6 +594,7 @@
     every_token = token_count * lax.axis_size("ctx")
     if exp_size == 2 and every_token <= 3 * expert_count * capacity:
         return dense_experts(
+            place,
             hidden_own,
             every_ids,
             top_count,

time: 198 us -> 194 us (0.980)
  waiting for transfers between devices: 53.1 us -> 44.3 us
  starting transfers between devices: 38.7 us -> 45.5 us
  other arithmetic: 10.4 us -> 7.27 us
    ppermute x19, starting transfers between devices: 16.2 us -> 22 us  [move(): lax.ppermute(value, 'ctx', [(i, partner(i)) for i in range(lax.axis_size(...]
    ppermute x19, waiting for transfers between devices: 30.1 us -> 25.2 us  [move(): lax.ppermute(value, 'ctx', [(i, partner(i)) for i in range(lax.axis_size(...]
    all_to_all x1, waiting for transfers between devices: 13.4 us -> 11.2 us  [exchange(): lax.all_to_all(array, 'ctx', split_axis=0, concat_axis=0, axis_index_grou...]
    unnamed x65 -> x79, local copies, waits for them, and re-layouts: 5.34 us -> 6.24 us
  transfers between devices with their start and end apart: 37 -> 37, of which waited for: 19 -> 18; matrix products, arithmetic and copies ran while one was open for 7% -> 5% of each run, Pallas kernels for 28% -> 29%
where the time goes in v3:
time: 194 us; the launch traced here: 193 us
  Pallas kernels  58.7 us (30%)
  starting transfers between devices  45.5 us (23%)
  waiting for transfers between devices  44.3 us (23%)
  blocking collectives  24.6 us (13%)
  local copies, waits for them, and re-layouts  12.3 us (6%)
  other arithmetic  7.27 us (4%)
    pallas_call x4, Pallas kernels, run_expert(): pl.pallas_call(functools.partial(expert_kernel, planes, top), out_shape=[...  44.1 us
    ppermute x19, waiting for transfers between devices, move(): lax.ppermute(value, 'ctx', [(i, partner(i)) for i in range(lax.axis_size(...  25.2 us
    all_to_all x1, blocking collectives, exchange(): lax.all_to_all(array, 'ctx', split_axis=0, concat_axis=0, axis_index_grou...  24.6 us
    ppermute x19, starting transfers between devices, move(): lax.ppermute(value, 'ctx', [(i, partner(i)) for i in range(lax.axis_size(...  22 us
    all_to_all x1, waiting for transfers between devices, exchange(): lax.all_to_all(array, 'ctx', split_axis=0, concat_axis=0, axis_index_grou...  11.2 us
    ppermute x8, starting transfers between devices, diagonal(): return lax.ppermute(value, ('ctx', 'exp'), pairs)  10.1 us
    ppermute x8, starting transfers between devices, across(): return lax.ppermute(value, 'exp', [(0, 1), (1, 0)])  8.29 us
    unnamed x79, local copies, waits for them, and re-layouts  6.24 us
  transfers between devices with their start and end apart: 37, of which 18 were waited for; matrix products, arithmetic and copies ran while one was open for 5% of the time, Pallas kernels for 29%

profile of v3, /device:TPU:0, one launch (start us, length us, event | category | flops | bytes accessed | tf_op | source)
XLA Modules:
  0.0 193.3 jit_solution(940906058465248326)
XLA Ops:
  8.3 24.6 %all_to_all.10.pairs = f32[8,152,128]{2,1,0:T(8,128)} all-to-all(f32[8,152,128]{2,1,0:T(8,128)S(1)} %fusion), channel_id=1, replica_groups={{0,4,8,12,16,20,24,28},{2,6,10,14,18,22,26,30},{1,5,9,13,17,21,25,29},{..., dimensions={0} | all-to-all | bytes 1245184 | tf_op jit(solution)/shard_map/all_to_all | solution.py:73
  32.9 2.1 %shard_map.146 = f32[8,128,128]{2,1,0:T(8,128)} custom-call(f32[8,152,128]{2,1,0:T(8,128)} %all_to_all.10.pairs), custom_call_target="tpu_custom_call" | custom-call | tf_op jit(solution)/shard_map/pallas_call | solution.py:78
  35.0 3.5 %all-to-all-start.1 = ((f32[8,128,128]{2,1,0:T(8,128)}), f32[8,128,128]{2,1,0:T(8,128)S(1)}, u32[]{:S(2)}, u32[]{:S(2)}) async-start(f32[8,128,128]{2,1,0:T(8,128)} %shard_map.146), calls=%async_computation.1 | async-start | bytes 1048576 | tf_op jit(solution)/shard_map/all_to_all | solution.py:73
  41.3 11.2 %all-to-all-done.1 = f32[8,128,128]{2,1,0:T(8,128)S(1)} async-done(((f32[8,128,128]{2,1,0:T(8,128)}), f32[8,128,128]{2,1,0:T(8,128)S(1)}, u32[]{:S(2)}, u32[]{:S(2)}) %all-to-all-start.1) | async-done | bytes 524320 | tf_op jit(solution)/shard_map/all_to_all | solution.py:73
  55.5 5.3 %shard_map.148 = (bf16[128,2048]{1,0:T(8,128)(2,1)}, bf16[1,128,1024]{2,1,0:T(8,128)(2,1)}) custom-call(s32[3]{0:T(128)} %pad_add_fusion.place, bf16[2048,2048]{1,0:T(8,128)(2,1)} %weight_hbm.3, f32[128,2048]{1,0:T(8,128)} %copy-done, f32[32,128]{1,0:T(8,128)} %copy-done.6, bf16[128,512]{1,0:T(8,128)(2,1)} %refs_2_.1, bf16[128,2048]{1,0:T(8,128)(2,1)} %refs_3_.1, ...), custom_call_target="tpu_custom_call" | custom-call | tf_op jit(solution)/shard_map/pallas_call | solution.py:555
  60.8 1.6 collective-permute-start.2
  62.4 4.9 %shard_map.149 = f32[128,1024]{1,0:T(8,128)} custom-call(s32[3]{0:T(128)} %pad_add_fusion.place, bf16[128,2048]{1,0:T(8,128)(2,1)} %get-tuple-element.85.normed, bf16[2048,2048]{1,0:T(8,128)(2,1)} %weight_hbm.3, bf16[128,1024]{1,0:T(8,128)(2,1)} %stream.1), custom_call_target="tpu_custom_call" | custom-call | flops 536870912 | bytes 4194304 | tf_op jit(solution)/shard_map/pallas_call | solution.py:573
  67.2 2.4 %collective-permute-done.2 = bf16[128,1024]{1,0:T(8,128)(2,1)S(1)} collective-permute-done((bf16[128,1024]{1,0:T(8,128)(2,1)}, bf16[128,1024]{1,0:T(8,128)(2,1)S(1)}, u32[]{:S(2)}, u32[]{:S(2)}) %collective-permute-start.2) | collective-permute-done | bytes 262176 | tf_op jit(solution)/shard_map/ppermute | solution.py:591
  73.8 4.6 %collective-permute-done.4.refs_2_ = bf16[128,1024]{1,0:T(8,128)(2,1)S(1)} collective-permute-done((bf16[128,1024]{1,0:T(8,128)(2,1)S(1)}, bf16[128,1024]{1,0:T(8,128)(2,1)S(1)}, u32[]{:S(2)}, u32[]{:S(2)}) %collective-permute-start.4) | collective-permute-done | bytes 262176 | tf_op jit(solution)/shard_map/ppermute | solution.py:16
  79.6 1.5 collective-permute-start.5
  89.9 11.0 %shard_map.150 = (bf16[128,1024]{1,0:T(8,128)(2,1)}, bf16[128,1024]{1,0:T(8,128)(2,1)}, bf16[128,1024]{1,0:T(8,128)(2,1)}, bf16[128,1024]{1,0:T(8,128)(2,1)}) custom-call(s32[3]{0:T(128)} %pad_add_fusion.place, bf16[128,1024]{1,0:T(8,128)(2,1)} %copy-done.10, bf16[128,1024]{1,0:T(8,128)(2,1)} %copy-done.13, bf16[128,1024]{1,0:T(8,128)(2,1)} %copy-done.12, ...), custom_call_target="tpu_custom_call" | custom-call | flops 4429185024 | bytes 19398656 | tf_op jit(solution)/shard_map/pallas_call | solution.py:188
  104.1 3.3 %collective-permute-start.16 = (bf16[128,1024]{1,0:T(8,128)(2,1)}, bf16[128,1024]{1,0:T(8,128)(2,1)S(1)}, u32[]{:S(2)}, u32[]{:S(2)}) collective-permute-start(bf16[128,1024]{1,0:T(8,128)(2,1)} %copy-done.10), channel_id=1, source_target_pairs={{0,8},{2,10},{4,12},{6,14},{8,16},{10,18},{12,20},{14,22},{16,24},... | collective-permute-start | bytes 786440 | tf_op jit(solution)/shard_map/ppermute | solution.py:16
  116.4 11.0 %shard_map.151 = (bf16[128,1024]{1,0:T(8,128)(2,1)}, bf16[128,1024]{1,0:T(8,128)(2,1)}, bf16[128,1024]{1,0:T(8,128)(2,1)}, bf16[128,1024]{1,0:T(8,128)(2,1)}) custom-call(s32[3]{0:T(128)} %pad_add_fusion.place, bf16[128,1024]{1,0:T(8,128)(2,1)} %copy-done.21, bf16[128,1024]{1,0:T(8,128)(2,1)} %copy-done.19, bf16[128,1024]{1,0:T(8,128)(2,1)} %copy-done.18, ...), custom_call_target="tpu_custom_call" | custom-call | flops 4429185024 | bytes 19398656 | tf_op jit(solution)/shard_map/pallas_call | solution.py:188
  130.3 1.7 collective-permute-start.24
  132.1 11.0 %shard_map.152 = (bf16[128,1024]{1,0:T(8,128)(2,1)}, bf16[128,1024]{1,0:T(8,128)(2,1)}, bf16[128,1024]{1,0:T(8,128)(2,1)}, bf16[128,1024]{1,0:T(8,128)(2,1)}) custom-call(s32[3]{0:T(128)} %pad_add_fusion.place, bf16[128,1024]{1,0:T(8,128)(2,1)} %copy-done.23, bf16[128,1024]{1,0:T(8,128)(2,1)} %copy-done.17, bf16[128,1024]{1,0:T(8,128)(2,1)} %copy-done.16, ...), custom_call_target="tpu_custom_call" | custom-call | flops 4429185024 | bytes 19398656 | tf_op jit(solution)/shard_map/pallas_call | solution.py:188
  145.9 11.0 %shard_map.153 = (bf16[128,1024]{1,0:T(8,128)(2,1)}, bf16[128,1024]{1,0:T(8,128)(2,1)}, bf16[128,1024]{1,0:T(8,128)(2,1)}, bf16[128,1024]{1,0:T(8,128)(2,1)}) custom-call(s32[3]{0:T(128)} %pad_add_fusion.place, bf16[128,1024]{1,0:T(8,128)(2,1)} %copy-done.22, bf16[128,1024]{1,0:T(8,128)(2,1)} %copy-done.15, bf16[128,1024]{1,0:T(8,128)(2,1)} %copy-done.14, ...), custom_call_target="tpu_custom_call" | custom-call | flops 4429185024 | bytes 19398656 | tf_op jit(solution)/shard_map/pallas_call | solution.py:188
  158.9 1.7 collective-permute-start.30
  160.8 3.4 %collective-permute-start.31 = (bf16[128,1024]{1,0:T(8,128)(2,1)S(1)}, bf16[128,1024]{1,0:T(8,128)(2,1)S(1)}, u32[]{:S(2)}, u32[]{:S(2)}) collective-permute-start(bf16[128,1024]{1,0:T(8,128)(2,1)S(1)} %add_convert_fusion.3), channel_id=1, source_target_pairs={{0,8},{2,10},{4,12},{6,14},{8,16},{10,18},{12,20},{14,22},{16,24},... | collective-permute-start | bytes 786440 | tf_op jit(solution)/shard_map/ppermute | solution.py:16
  165.0 3.2 %collective-permute-done.30 = bf16[128,1024]{1,0:T(8,128)(2,1)S(1)} collective-permute-done((bf16[128,1024]{1,0:T(8,128)(2,1)}, bf16[128,1024]{1,0:T(8,128)(2,1)S(1)}, u32[]{:S(2)}, u32[]{:S(2)}) %collective-permute-start.30) | collective-permute-done | bytes 262176 | tf_op jit(solution)/shard_map/ppermute | solution.py:229
  168.2 3.2 %collective-permute-done.31 = bf16[128,1024]{1,0:T(8,128)(2,1)S(1)} collective-permute-done((bf16[128,1024]{1,0:T(8,128)(2,1)S(1)}, bf16[128,1024]{1,0:T(8,128)(2,1)S(1)}, u32[]{:S(2)}, u32[]{:S(2)}) %collective-permute-start.31) | collective-permute-done | bytes 262176 | tf_op jit(solution)/shard_map/ppermute | solution.py:16
  174.7 4.2 %collective-permute-done.33 = bf16[128,1024]{1,0:T(8,128)(2,1)S(1)} collective-permute-done((bf16[128,1024]{1,0:T(8,128)(2,1)S(1)}, bf16[128,1024]{1,0:T(8,128)(2,1)S(1)}, u32[]{:S(2)}, u32[]{:S(2)}) %collective-permute-start.33) | collective-permute-done | bytes 262176 | tf_op jit(solution)/shard_map/ppermute | solution.py:16
  179.0 5.4 %collective-permute-done.34 = bf16[128,1024]{1,0:T(8,128)(2,1)S(1)} collective-permute-done((bf16[128,1024]{1,0:T(8,128)(2,1)S(1)}, bf16[128,1024]{1,0:T(8,128)(2,1)S(1)}, u32[]{:S(2)}, u32[]{:S(2)}) %collective-permute-start.34) | collective-permute-done | bytes 262176 | tf_op jit(solution)/shard_map/ppermute | solution.py:16
  184.6 3.8 %collective-permute-start.35 = (bf16[128,1024]{1,0:T(8,128)(2,1)S(1)}, bf16[128,1024]{1,0:T(8,128)(2,1)S(1)}, u32[]{:S(2)}, u32[]{:S(2)}) collective-permute-start(bf16[128,1024]{1,0:T(8,128)(2,1)S(1)} %add_convert_fusion.1), channel_id=1, source_target_pairs={{0,24},{2,26},{4,28},{6,30},{8,0},{10,2},{12,4},{14,6},{16,8},{18,... | collective-permute-start | bytes 786440 | tf_op jit(solution)/shard_map/ppermute | solution.py:16
  188.4 3.9 %collective-permute-done.35 = bf16[128,1024]{1,0:T(8,128)(2,1)S(1)} collective-permute-done((bf16[128,1024]{1,0:T(8,128)(2,1)S(1)}, bf16[128,1024]{1,0:T(8,128)(2,1)S(1)}, u32[]{:S(2)}, u32[]{:S(2)}) %collective-permute-start.35) | collective-permute-done | bytes 262176 | tf_op jit(solution)/shard_map/ppermute | solution.py:16
  (188 shorter events, 53.0 us)
Async XLA Ops:
  35.0 17.5 %all-to-all-start.1 = ((f32[8,128,128]{2,1,0:T(8,128)}), f32[8,128,128]{2,1,0:T(8,128)S(1)}, u32[]{:S(2)}, u32[]{:S(2)}) async-start(f32[8,128,128]{2,1,0:T(8,128)} %shard_map.146), calls=%async_computation.1 | async-start | bytes 1048576 | tf_op jit(solution)/shard_map/all_to_all | solution.py:73
  38.5 50.9 %collective-permute-start.7 = (bf16[704,2048]{1,0:T(8,128)(2,1)}, bf16[704,2048]{1,0:T(8,128)(2,1)}, u32[]{:S(2)}, u32[]{:S(2)}) collective-permute-start(bf16[704,2048]{1,0:T(8,128)(2,1)} %bitcast.41), channel_id=1, source_target_pairs={{0,2},{2,0},{4,6},{6,4},{8,10},{10,8},{12,14},{14,12},{16,18},{18,... | collective-permute-start | bytes 8650760 | tf_op jit(solution)/shard_map/ppermute | solution.py:16
  38.6 51.3 %collective-permute-start.8 = (bf16[704,2048]{1,0:T(8,128)(2,1)}, bf16[704,2048]{1,0:T(8,128)(2,1)}, u32[]{:S(2)}, u32[]{:S(2)}) collective-permute-start(bf16[704,2048]{1,0:T(8,128)(2,1)} %bitcast.46), channel_id=1, source_target_pairs={{0,2},{2,0},{4,6},{6,4},{8,10},{10,8},{12,14},{14,12},{16,18},{18,... | collective-permute-start | bytes 8650760 | tf_op jit(solution)/shard_map/ppermute | solution.py:16
  39.1 50.8 %collective-permute-start.9 = (bf16[704,2048]{1,0:T(8,128)(2,1)}, bf16[704,2048]{1,0:T(8,128)(2,1)}, u32[]{:S(2)}, u32[]{:S(2)}) collective-permute-start(bf16[704,2048]{1,0:T(8,128)(2,1)} %bitcast.51), channel_id=1, source_target_pairs={{0,2},{2,0},{4,6},{6,4},{8,10},{10,8},{12,14},{14,12},{16,18},{18,... | collective-permute-start | bytes 8650760 | tf_op jit(solution)/shard_map/ppermute | solution.py:16
  87.5 14.0 %collective-permute-start.11 = (bf16[128,1024]{1,0:T(8,128)(2,1)S(1)}, bf16[128,1024]{1,0:T(8,128)(2,1)S(1)}, u32[]{:S(2)}, u32[]{:S(2)}) collective-permute-start(bf16[128,1024]{1,0:T(8,128)(2,1)S(1)} %collective-permute-done.6.refs_0_), channel_id=1, source_target_pairs={{0,4},{2,6},{4,0},{6,2},{8,12},{10,14},{12,8},{14,10},{16,20},{18,... | collective-permute-start | bytes 786440 | tf_op jit(solution)/shard_map/ppermute | solution.py:16
  88.2 13.4 %collective-permute-start.10 = (bf16[128,1024]{1,0:T(8,128)(2,1)S(1)}, bf16[128,1024]{1,0:T(8,128)(2,1)S(1)}, u32[]{:S(2)}, u32[]{:S(2)}) collective-permute-start(bf16[128,1024]{1,0:T(8,128)(2,1)S(1)} %collective-permute-done.6.refs_0_), channel_id=1, source_target_pairs={{0,1},{1,0},{2,3},{3,2},{4,5},{5,4},{6,7},{7,6},{8,9},{9,8},{10,11... | collective-permute-start | bytes 786440 | tf_op jit(solution)/shard_map/ppermute | solution.py:221
  89.4 12.1 %collective-permute-start.12 = (bf16[128,1024]{1,0:T(8,128)(2,1)S(1)}, bf16[128,1024]{1,0:T(8,128)(2,1)S(1)}, u32[]{:S(2)}, u32[]{:S(2)}) collective-permute-start(bf16[128,1024]{1,0:T(8,128)(2,1)S(1)} %add_convert_fusion.4.refs_0_), channel_id=1, source_target_pairs={{0,16},{2,18},{4,20},{6,22},{8,24},{10,26},{12,28},{14,30},{16,0},... | collective-permute-start | bytes 786440 | tf_op jit(solution)/shard_map/ppermute | solution.py:16
  101.5 11.1 %collective-permute-start.15 = (bf16[128,1024]{1,0:T(8,128)(2,1)S(1)}, bf16[128,1024]{1,0:T(8,128)(2,1)S(1)}, u32[]{:S(2)}, u32[]{:S(2)}) collective-permute-start(bf16[128,1024]{1,0:T(8,128)(2,1)S(1)} %collective-permute-done.12.refs_0_), channel_id=1, source_target_pairs={{0,4},{2,6},{4,0},{6,2},{8,12},{10,14},{12,8},{14,10},{16,20},{18,... | collective-permute-start | bytes 786440 | tf_op jit(solution)/shard_map/ppermute | solution.py:16
  101.9 10.7 %collective-permute-start.14 = (bf16[128,1024]{1,0:T(8,128)(2,1)S(1)}, bf16[128,1024]{1,0:T(8,128)(2,1)S(1)}, u32[]{:S(2)}, u32[]{:S(2)}) collective-permute-start(bf16[128,1024]{1,0:T(8,128)(2,1)S(1)} %collective-permute-done.12.refs_0_), channel_id=1, source_target_pairs={{0,1},{1,0},{2,3},{3,2},{4,5},{5,4},{6,7},{7,6},{8,9},{9,8},{10,11... | collective-permute-start | bytes 786440 | tf_op jit(solution)/shard_map/ppermute | solution.py:221
  103.5 8.9 %collective-permute-start.13 = (bf16[128,1024]{1,0:T(8,128)(2,1)S(1)}, bf16[128,1024]{1,0:T(8,128)(2,1)S(1)}, u32[]{:S(2)}, u32[]{:S(2)}) collective-permute-start(bf16[128,1024]{1,0:T(8,128)(2,1)S(1)} %broadcast_select_fusion.2), channel_id=1, source_target_pairs={{0,1},{1,0},{2,6},{3,7},{4,5},{5,4},{6,2},{7,3},{8,9},{9,8},{10,14... | collective-permute-start | bytes 786440 | tf_op jit(solution)/shard_map/ppermute | solution.py:229
  110.9 16.6 %collective-permute-start.20 = (bf16[128,1024]{1,0:T(8,128)(2,1)}, bf16[128,1024]{1,0:T(8,128)(2,1)S(1)}, u32[]{:S(2)}, u32[]{:S(2)}) collective-permute-start(bf16[128,1024]{1,0:T(8,128)(2,1)} %get-tuple-element.110), channel_id=1, source_target_pairs={{0,1},{1,0},{2,6},{3,7},{4,5},{5,4},{6,2},{7,3},{8,9},{9,8},{10,14... | collective-permute-start | bytes 786440 | tf_op jit(solution)/shard_map/ppermute | solution.py:229
  112.7 14.8 %collective-permute-start.18 = (bf16[128,1024]{1,0:T(8,128)(2,1)S(1)}, bf16[128,1024]{1,0:T(8,128)(2,1)S(1)}, u32[]{:S(2)}, u32[]{:S(2)}) collective-permute-start(bf16[128,1024]{1,0:T(8,128)(2,1)S(1)} %collective-permute-done.16.refs_0_), channel_id=1, source_target_pairs={{0,4},{2,6},{4,0},{6,2},{8,12},{10,14},{12,8},{14,10},{16,20},{18,... | collective-permute-start | bytes 786440 | tf_op jit(solution)/shard_map/ppermute | solution.py:16
  114.2 13.3 %collective-permute-start.17 = (bf16[128,1024]{1,0:T(8,128)(2,1)S(1)}, bf16[128,1024]{1,0:T(8,128)(2,1)S(1)}, u32[]{:S(2)}, u32[]{:S(2)}) collective-permute-start(bf16[128,1024]{1,0:T(8,128)(2,1)S(1)} %collective-permute-done.16.refs_0_), channel_id=1, source_target_pairs={{0,1},{1,0},{2,3},{3,2},{4,5},{5,4},{6,7},{7,6},{8,9},{9,8},{10,11... | collective-permute-start | bytes 786440 | tf_op jit(solution)/shard_map/ppermute | solution.py:221
  115.1 12.3 %collective-permute-start.19 = (bf16[128,1024]{1,0:T(8,128)(2,1)S(1)}, bf16[128,1024]{1,0:T(8,128)(2,1)S(1)}, u32[]{:S(2)}, u32[]{:S(2)}) collective-permute-start(bf16[128,1024]{1,0:T(8,128)(2,1)S(1)} %broadcast_select_fusion.1), channel_id=1, source_target_pairs={{0,1},{1,0},{2,6},{3,7},{4,5},{5,4},{6,2},{7,3},{8,9},{9,8},{10,14... | collective-permute-start | bytes 786440 | tf_op jit(solution)/shard_map/ppermute | solution.py:229
  127.6 15.6 %collective-permute-start.21 = (bf16[128,1024]{1,0:T(8,128)(2,1)S(1)}, bf16[128,1024]{1,0:T(8,128)(2,1)S(1)}, u32[]{:S(2)}, u32[]{:S(2)}) collective-permute-start(bf16[128,1024]{1,0:T(8,128)(2,1)S(1)} %broadcast_select_fusion), channel_id=1, source_target_pairs={{0,1},{1,0},{2,6},{3,7},{4,5},{5,4},{6,2},{7,3},{8,9},{9,8},{10,14... | collective-permute-start | bytes 786440 | tf_op jit(solution)/shard_map/ppermute | solution.py:229
  128.5 14.6 %collective-permute-start.23 = (bf16[128,1024]{1,0:T(8,128)(2,1)S(1)}, bf16[128,1024]{1,0:T(8,128)(2,1)S(1)}, u32[]{:S(2)}, u32[]{:S(2)}) collective-permute-start(bf16[128,1024]{1,0:T(8,128)(2,1)S(1)} %get-tuple-element.167), channel_id=1, source_target_pairs={{0,4},{2,6},{4,0},{6,2},{8,12},{10,14},{12,8},{14,10},{16,20},{18,... | collective-permute-start | bytes 786440 | tf_op jit(solution)/shard_map/ppermute | solution.py:16
  130.1 13.1 %collective-permute-start.22 = (bf16[128,1024]{1,0:T(8,128)(2,1)S(1)}, bf16[128,1024]{1,0:T(8,128)(2,1)S(1)}, u32[]{:S(2)}, u32[]{:S(2)}) collective-permute-start(bf16[128,1024]{1,0:T(8,128)(2,1)S(1)} %get-tuple-element.168), channel_id=1, source_target_pairs={{0,1},{1,0},{2,3},{3,2},{4,5},{5,4},{6,7},{7,6},{8,9},{9,8},{10,11... | collective-permute-start | bytes 786440 | tf_op jit(solution)/shard_map/ppermute | solution.py:221
  130.3 12.8 %collective-permute-start.24 = (bf16[128,1024]{1,0:T(8,128)(2,1)}, bf16[128,1024]{1,0:T(8,128)(2,1)S(1)}, u32[]{:S(2)}, u32[]{:S(2)}) collective-permute-start(bf16[128,1024]{1,0:T(8,128)(2,1)} %get-tuple-element.121), channel_id=1, source_target_pairs={{0,1},{1,0},{2,6},{3,7},{4,5},{5,4},{6,2},{7,3},{8,9},{9,8},{10,14... | collective-permute-start | bytes 786440 | tf_op jit(solution)/shard_map/ppermute | solution.py:229
  143.3 13.7 %collective-permute-start.26 = (bf16[128,1024]{1,0:T(8,128)(2,1)S(1)}, bf16[128,1024]{1,0:T(8,128)(2,1)S(1)}, u32[]{:S(2)}, u32[]{:S(2)}) collective-permute-start(bf16[128,1024]{1,0:T(8,128)(2,1)S(1)} %get-tuple-element.165), channel_id=1, source_target_pairs={{0,4},{2,6},{4,0},{6,2},{8,12},{10,14},{12,8},{14,10},{16,20},{18,... | collective-permute-start | bytes 786440 | tf_op jit(solution)/shard_map/ppermute | solution.py:16
  143.9 13.1 %collective-permute-start.25 = (bf16[128,1024]{1,0:T(8,128)(2,1)S(1)}, bf16[128,1024]{1,0:T(8,128)(2,1)S(1)}, u32[]{:S(2)}, u32[]{:S(2)}) collective-permute-start(bf16[128,1024]{1,0:T(8,128)(2,1)S(1)} %get-tuple-element.166), channel_id=1, source_target_pairs={{0,1},{1,0},{2,3},{3,2},{4,5},{5,4},{6,7},{7,6},{8,9},{9,8},{10,11... | collective-permute-start | bytes 786440 | tf_op jit(solution)/shard_map/ppermute | solution.py:221
  145.1 11.9 %collective-permute-start.27 = (bf16[128,1024]{1,0:T(8,128)(2,1)}, bf16[128,1024]{1,0:T(8,128)(2,1)S(1)}, u32[]{:S(2)}, u32[]{:S(2)}) collective-permute-start(bf16[128,1024]{1,0:T(8,128)(2,1)} %get-tuple-element.133), channel_id=1, source_target_pairs={{0,1},{1,0},{2,6},{3,7},{4,5},{5,4},{6,2},{7,3},{8,9},{9,8},{10,14... | collective-permute-start | bytes 786440 | tf_op jit(solution)/shard_map/ppermute | solution.py:229
  158.9 9.3 %collective-permute-start.30 = (bf16[128,1024]{1,0:T(8,128)(2,1)}, bf16[128,1024]{1,0:T(8,128)(2,1)S(1)}, u32[]{:S(2)}, u32[]{:S(2)}) collective-permute-start(bf16[128,1024]{1,0:T(8,128)(2,1)} %get-tuple-element.136), channel_id=1, source_target_pairs={{0,1},{1,0},{2,6},{3,7},{4,5},{5,4},{6,2},{7,3},{8,9},{9,8},{10,14... | collective-permute-start | bytes 786440 | tf_op jit(solution)/shard_map/ppermute | solution.py:229
  160.8 10.6 %collective-permute-start.31 = (bf16[128,1024]{1,0:T(8,128)(2,1)S(1)}, bf16[128,1024]{1,0:T(8,128)(2,1)S(1)}, u32[]{:S(2)}, u32[]{:S(2)}) collective-permute-start(bf16[128,1024]{1,0:T(8,128)(2,1)S(1)} %add_convert_fusion.3), channel_id=1, source_target_pairs={{0,8},{2,10},{4,12},{6,14},{8,16},{10,18},{12,20},{14,22},{16,24},... | collective-permute-start | bytes 786440 | tf_op jit(solution)/shard_map/ppermute | solution.py:16
  174.2 10.3 %collective-permute-start.34 = (bf16[128,1024]{1,0:T(8,128)(2,1)S(1)}, bf16[128,1024]{1,0:T(8,128)(2,1)S(1)}, u32[]{:S(2)}, u32[]{:S(2)}) collective-permute-start(bf16[128,1024]{1,0:T(8,128)(2,1)S(1)} %add_convert_fusion.2), channel_id=1, source_target_pairs={{0,16},{2,18},{4,20},{6,22},{8,24},{10,26},{12,28},{14,30},{16,0},... | collective-permute-start | bytes 786440 | tf_op jit(solution)/shard_map/ppermute | solution.py:16
  (52 other events, 678.7 us)

commit v4 on v3

--- a/solution.py
+++ b/solution.py
@@ -79,7 +79,7 @@
         chain_kernel, out_shape=jax.ShapeDtypeStruct((size // 2, share, width), jnp.float32)
     )(pairs)
     into_first = exchange(found).reshape(half, width)
-    into_first, beside = lax.optimization_barrier((into_first, beside))
+    into_first, *beside = lax.optimization_barrier((into_first, *beside))
     into_second = jnp.exp(first_log)[:, None] * into_first + first
     back = move(pick(odd, into_second, into_first), lambda i: i ^ 1)
     into_first, first, first_log = lax.optimization_barrier((into_first, first, first_log))
@@ -238,9 +238,9 @@
         [("diag", 0), ("z", 1)],
         [("K", 0), ("x", 1), ("y", 1), ("z", 2)],
         [("diag", 1), ("x", 2), ("y", 2), ("z", 3)],
-        [("K", 1), ("x", 3), ("y", 3), ("diag", 2), ("rdiag", 0)],
-        [("K", 2), ("diag", 3), ("rx", 0), ("ry", 0), ("rdiag", 1)],
-        [("K", 3), ("rx", 1), ("ry", 1), ("rdiag", 2)],
+        [("K", 1), ("x", 3), ("y", 3), ("diag", 2)],
+        [("K", 2), ("diag", 3), ("rdiag", 0), ("rdiag", 1)],
+        [("K", 3), ("rx", 0), ("ry", 0), ("rx", 1), ("ry", 1), ("rdiag", 2)],
         [("rx", 2), ("ry", 2), ("rdiag", 3), ("rz", 1)],
         [("rx", 3), ("ry", 3), ("rz", 2)],
         [("rz", 3)],
@@ -284,7 +284,7 @@
                 for flips in (0, 2)
             ]
         )
-        return run_expert(place, values, every_ids[order], top, moe_gain[None], router, weights)
+        return run_expert(place, values, every_ids[order], top, moe_gain, router, weights)
 
     for phase in phases:
         outs = [run(*step, operands(*step)) for step in phase]
@@ -540,9 +540,11 @@
             transcendentals=head_count * token_count * token_count,
         ),
     )(step_size, running, ssm_input, b_input, c_input)
-    mine, back, inner, every_ids = prefix_states(state, running[:, -1], id_rows, inner)
     here = lax.axis_index("ctx")
     place = jnp.stack([here, lax.axis_index("exp"), here ^ 1]).astype(jnp.int32)
+    beside = (inner, place, norm_gain[None], moe_gain[None])
+    mine, back, beside, every_ids = prefix_states(state, running[:, -1], id_rows, beside)
+    inner, place, norm_row, moe_row = beside
     fetched = (
         inner,
         running,
@@ -550,7 +552,7 @@
         gate_input,
         mine,
         back,
-        norm_gain[None],
+        norm_row,
     )
     normed, theirs = pl.pallas_call(
         mixer_kernel,
@@ -592,13 +594,14 @@
         hidden_own = hidden_own + sent.astype(jnp.float32)
     hidden_own = hidden_own.astype(jnp.bfloat16)
     every_token = token_count * lax.axis_size("ctx")
-    if exp_size == 2 and every_token <= 3 * expert_count * capacity:
+    planes = lax.axis_size("ctx") // PLANE
+    if exp_size == 2 and planes == 4 and every_token <= 3 * expert_count * capacity:
         return dense_experts(
             place,
             hidden_own,
             every_ids,
             top_count,
-            moe_gain,
+            moe_row,
             router,
             (w_gate[0], w_up[0], w_down[0]),
         )

time: 194 us -> 194 us (level)
  starting transfers between devices: 45.5 us -> 50 us
  waiting for transfers between devices: 44.3 us -> 39.8 us
    ppermute x19, starting transfers between devices: 22 us -> 27.3 us  [move(): lax.ppermute(value, 'ctx', [(i, partner(i)) for i in range(lax.axis_size(...]
    ppermute x19, waiting for transfers between devices: 25.2 us -> 20.4 us  [move(): lax.ppermute(value, 'ctx', [(i, partner(i)) for i in range(lax.axis_size(...]
  transfers between devices with their start and end apart: 37 -> 37, of which waited for: 18 -> 15; matrix products, arithmetic and copies ran while one was open for 5% -> 5% of each run, Pallas kernels for 29% -> 29%
where the time goes in v4:
time: 194 us; the launch traced here: 193 us
  Pallas kernels  58.7 us (30%)
  starting transfers between devices  50 us (26%)
  waiting for transfers between devices  39.8 us (21%)
  blocking collectives  24.6 us (13%)
  local copies, waits for them, and re-layouts  12.3 us (6%)
  other arithmetic  7.19 us (4%)
    pallas_call x4, Pallas kernels, run_expert(): pl.pallas_call(functools.partial(expert_kernel, planes, top), out_shape=[...  44.1 us
    ppermute x19, starting transfers between devices, move(): lax.ppermute(value, 'ctx', [(i, partner(i)) for i in range(lax.axis_size(...  27.3 us
    all_to_all x1, blocking collectives, exchange(): lax.all_to_all(array, 'ctx', split_axis=0, concat_axis=0, axis_index_grou...  24.6 us
    ppermute x19, waiting for transfers between devices, move(): lax.ppermute(value, 'ctx', [(i, partner(i)) for i in range(lax.axis_size(...  20.4 us
    all_to_all x1, waiting for transfers between devices, exchange(): lax.all_to_all(array, 'ctx', split_axis=0, concat_axis=0, axis_index_grou...  10.7 us
    ppermute x8, starting transfers between devices, diagonal(): return lax.ppermute(value, ('ctx', 'exp'), pairs)  9.32 us
    ppermute x8, starting transfers between devices, across(): return lax.ppermute(value, 'exp', [(0, 1), (1, 0)])  8.33 us
    unnamed x79, local copies, waits for them, and re-layouts  6.24 us
  transfers between devices with their start and end apart: 37, of which 15 were waited for; matrix products, arithmetic and copies ran while one was open for 5% of the time, Pallas kernels for 29%

profile of v4, /device:TPU:0, one launch (start us, length us, event | category | flops | bytes accessed | tf_op | source)
XLA Modules:
  0.0 193.3 jit_solution(7527442044065362131)
XLA Ops:
  8.3 24.6 %all_to_all.10.pairs = f32[8,152,128]{2,1,0:T(8,128)} all-to-all(f32[8,152,128]{2,1,0:T(8,128)S(1)} %fusion), channel_id=1, replica_groups={{0,4,8,12,16,20,24,28},{2,6,10,14,18,22,26,30},{1,5,9,13,17,21,25,29},{..., dimensions={0} | all-to-all | bytes 1245184 | tf_op jit(solution)/shard_map/all_to_all | solution.py:73
  32.9 2.1 %shard_map.146 = f32[8,128,128]{2,1,0:T(8,128)} custom-call(f32[8,152,128]{2,1,0:T(8,128)} %all_to_all.10.pairs), custom_call_target="tpu_custom_call" | custom-call | tf_op jit(solution)/shard_map/pallas_call | solution.py:78
  35.0 3.5 %all-to-all-start.1 = ((f32[8,128,128]{2,1,0:T(8,128)}), f32[8,128,128]{2,1,0:T(8,128)S(1)}, u32[]{:S(2)}, u32[]{:S(2)}) async-start(f32[8,128,128]{2,1,0:T(8,128)} %shard_map.146), calls=%async_computation.1 | async-start | bytes 1048576 | tf_op jit(solution)/shard_map/all_to_all | solution.py:73
  41.9 10.7 %all-to-all-done.1 = f32[8,128,128]{2,1,0:T(8,128)S(1)} async-done(((f32[8,128,128]{2,1,0:T(8,128)}), f32[8,128,128]{2,1,0:T(8,128)S(1)}, u32[]{:S(2)}, u32[]{:S(2)}) %all-to-all-start.1) | async-done | bytes 524320 | tf_op jit(solution)/shard_map/all_to_all | solution.py:73
  55.5 5.3 %shard_map.148 = (bf16[128,2048]{1,0:T(8,128)(2,1)}, bf16[1,128,1024]{2,1,0:T(8,128)(2,1)}) custom-call(s32[3]{0:T(128)} %pad_add_fusion.place, bf16[2048,2048]{1,0:T(8,128)(2,1)} %weight_hbm.3, f32[128,2048]{1,0:T(8,128)} %copy-done, f32[32,128]{1,0:T(8,128)} %copy-done.6, bf16[128,512]{1,0:T(8,128)(2,1)} %refs_2_.1, bf16[128,2048]{1,0:T(8,128)(2,1)} %refs_3_.1, ...), custom_call_target="tpu_custom_call" | custom-call | tf_op jit(solution)/shard_map/pallas_call | solution.py:557
  60.8 1.6 collective-permute-start.2
  62.4 4.9 %shard_map.149 = f32[128,1024]{1,0:T(8,128)} custom-call(s32[3]{0:T(128)} %pad_add_fusion.place, bf16[128,2048]{1,0:T(8,128)(2,1)} %get-tuple-element.90.normed, bf16[2048,2048]{1,0:T(8,128)(2,1)} %weight_hbm.3, bf16[128,1024]{1,0:T(8,128)(2,1)} %stream.1), custom_call_target="tpu_custom_call" | custom-call | flops 536870912 | bytes 4194304 | tf_op jit(solution)/shard_map/pallas_call | solution.py:575
  67.2 2.2 %collective-permute-done.2 = bf16[128,1024]{1,0:T(8,128)(2,1)S(1)} collective-permute-done((bf16[128,1024]{1,0:T(8,128)(2,1)}, bf16[128,1024]{1,0:T(8,128)(2,1)S(1)}, u32[]{:S(2)}, u32[]{:S(2)}) %collective-permute-start.2) | collective-permute-done | bytes 262176 | tf_op jit(solution)/shard_map/ppermute | solution.py:593
  73.7 4.5 %collective-permute-done.4.refs_2_ = bf16[128,1024]{1,0:T(8,128)(2,1)S(1)} collective-permute-done((bf16[128,1024]{1,0:T(8,128)(2,1)S(1)}, bf16[128,1024]{1,0:T(8,128)(2,1)S(1)}, u32[]{:S(2)}, u32[]{:S(2)}) %collective-permute-start.4) | collective-permute-done | bytes 262176 | tf_op jit(solution)/shard_map/ppermute | solution.py:16
  79.3 1.5 collective-permute-start.5
  80.8 1.9 collective-permute-start.6
  89.9 11.1 %shard_map.150 = (bf16[128,1024]{1,0:T(8,128)(2,1)}, bf16[128,1024]{1,0:T(8,128)(2,1)}, bf16[128,1024]{1,0:T(8,128)(2,1)}, bf16[128,1024]{1,0:T(8,128)(2,1)}) custom-call(s32[3]{0:T(128)} %pad_add_fusion.place, bf16[128,1024]{1,0:T(8,128)(2,1)} %copy-done.10, bf16[128,1024]{1,0:T(8,128)(2,1)} %copy-done.13, bf16[128,1024]{1,0:T(8,128)(2,1)} %copy-done.12, ...), custom_call_target="tpu_custom_call" | custom-call | flops 4429185024 | bytes 19398656 | tf_op jit(solution)/shard_map/pallas_call | solution.py:188
  104.1 3.3 %collective-permute-start.16 = (bf16[128,1024]{1,0:T(8,128)(2,1)}, bf16[128,1024]{1,0:T(8,128)(2,1)S(1)}, u32[]{:S(2)}, u32[]{:S(2)}) collective-permute-start(bf16[128,1024]{1,0:T(8,128)(2,1)} %copy-done.10), channel_id=1, source_target_pairs={{0,8},{2,10},{4,12},{6,14},{8,16},{10,18},{12,20},{14,22},{16,24},... | collective-permute-start | bytes 786440 | tf_op jit(solution)/shard_map/ppermute | solution.py:16
  115.9 11.0 %shard_map.151 = (bf16[128,1024]{1,0:T(8,128)(2,1)}, bf16[128,1024]{1,0:T(8,128)(2,1)}, bf16[128,1024]{1,0:T(8,128)(2,1)}, bf16[128,1024]{1,0:T(8,128)(2,1)}) custom-call(s32[3]{0:T(128)} %pad_add_fusion.place, bf16[128,1024]{1,0:T(8,128)(2,1)} %copy-done.21, bf16[128,1024]{1,0:T(8,128)(2,1)} %copy-done.17, bf16[128,1024]{1,0:T(8,128)(2,1)} %copy-done.16, ...), custom_call_target="tpu_custom_call" | custom-call | flops 4429185024 | bytes 19398656 | tf_op jit(solution)/shard_map/pallas_call | solution.py:188
  129.2 11.0 %shard_map.152 = (bf16[128,1024]{1,0:T(8,128)(2,1)}, bf16[128,1024]{1,0:T(8,128)(2,1)}, bf16[128,1024]{1,0:T(8,128)(2,1)}, bf16[128,1024]{1,0:T(8,128)(2,1)}) custom-call(s32[3]{0:T(128)} %pad_add_fusion.place, bf16[128,1024]{1,0:T(8,128)(2,1)} %copy-done.23, bf16[128,1024]{1,0:T(8,128)(2,1)} %copy-done.19, bf16[128,1024]{1,0:T(8,128)(2,1)} %copy-done.18, ...), custom_call_target="tpu_custom_call" | custom-call | flops 4429185024 | bytes 19398656 | tf_op jit(solution)/shard_map/pallas_call | solution.py:188
  141.2 1.5 collective-permute-start.25
  145.5 11.0 %shard_map.153 = (bf16[128,1024]{1,0:T(8,128)(2,1)}, bf16[128,1024]{1,0:T(8,128)(2,1)}, bf16[128,1024]{1,0:T(8,128)(2,1)}, bf16[128,1024]{1,0:T(8,128)(2,1)}) custom-call(s32[3]{0:T(128)} %pad_add_fusion.place, bf16[128,1024]{1,0:T(8,128)(2,1)} %copy-done.22, bf16[128,1024]{1,0:T(8,128)(2,1)} %copy-done.15, bf16[128,1024]{1,0:T(8,128)(2,1)} %copy-done.14, ...), custom_call_target="tpu_custom_call" | custom-call | flops 4429185024 | bytes 19398656 | tf_op jit(solution)/shard_map/pallas_call | solution.py:188
  156.7 1.5 collective-permute-start.29
  160.4 3.8 %collective-permute-start.31 = (bf16[128,1024]{1,0:T(8,128)(2,1)S(1)}, bf16[128,1024]{1,0:T(8,128)(2,1)S(1)}, u32[]{:S(2)}, u32[]{:S(2)}) collective-permute-start(bf16[128,1024]{1,0:T(8,128)(2,1)S(1)} %add_convert_fusion.3), channel_id=1, source_target_pairs={{0,8},{2,10},{4,12},{6,14},{8,16},{10,18},{12,20},{14,22},{16,24},... | collective-permute-start | bytes 786440 | tf_op jit(solution)/shard_map/ppermute | solution.py:16
  164.6 4.0 %collective-permute-done.30 = bf16[128,1024]{1,0:T(8,128)(2,1)S(1)} collective-permute-done((bf16[128,1024]{1,0:T(8,128)(2,1)}, bf16[128,1024]{1,0:T(8,128)(2,1)S(1)}, u32[]{:S(2)}, u32[]{:S(2)}) %collective-permute-start.30) | collective-permute-done | bytes 262176 | tf_op jit(solution)/shard_map/ppermute | solution.py:229
  172.5 3.8 %collective-permute-start.34 = (bf16[128,1024]{1,0:T(8,128)(2,1)S(1)}, bf16[128,1024]{1,0:T(8,128)(2,1)S(1)}, u32[]{:S(2)}, u32[]{:S(2)}) collective-permute-start(bf16[128,1024]{1,0:T(8,128)(2,1)S(1)} %add_convert_fusion.2), channel_id=1, source_target_pairs={{0,16},{2,18},{4,20},{6,22},{8,24},{10,26},{12,28},{14,30},{16,0},... | collective-permute-start | bytes 786440 | tf_op jit(solution)/shard_map/ppermute | solution.py:16
  178.5 6.0 %collective-permute-done.34 = bf16[128,1024]{1,0:T(8,128)(2,1)S(1)} collective-permute-done((bf16[128,1024]{1,0:T(8,128)(2,1)S(1)}, bf16[128,1024]{1,0:T(8,128)(2,1)S(1)}, u32[]{:S(2)}, u32[]{:S(2)}) %collective-permute-start.34) | collective-permute-done | bytes 262176 | tf_op jit(solution)/shard_map/ppermute | solution.py:16
  184.6 3.8 %collective-permute-start.35 = (bf16[128,1024]{1,0:T(8,128)(2,1)S(1)}, bf16[128,1024]{1,0:T(8,128)(2,1)S(1)}, u32[]{:S(2)}, u32[]{:S(2)}) collective-permute-start(bf16[128,1024]{1,0:T(8,128)(2,1)S(1)} %add_convert_fusion.1), channel_id=1, source_target_pairs={{0,24},{2,26},{4,28},{6,30},{8,0},{10,2},{12,4},{14,6},{16,8},{18,... | collective-permute-start | bytes 786440 | tf_op jit(solution)/shard_map/ppermute | solution.py:16
  188.4 3.9 %collective-permute-done.35 = bf16[128,1024]{1,0:T(8,128)(2,1)S(1)} collective-permute-done((bf16[128,1024]{1,0:T(8,128)(2,1)S(1)}, bf16[128,1024]{1,0:T(8,128)(2,1)S(1)}, u32[]{:S(2)}, u32[]{:S(2)}) %collective-permute-start.35) | collective-permute-done | bytes 262176 | tf_op jit(solution)/shard_map/ppermute | solution.py:16
  (188 shorter events, 54.3 us)
Async XLA Ops:
  35.0 17.5 %all-to-all-start.1 = ((f32[8,128,128]{2,1,0:T(8,128)}), f32[8,128,128]{2,1,0:T(8,128)S(1)}, u32[]{:S(2)}, u32[]{:S(2)}) async-start(f32[8,128,128]{2,1,0:T(8,128)} %shard_map.146), calls=%async_computation.1 | async-start | bytes 1048576 | tf_op jit(solution)/shard_map/all_to_all | solution.py:73
  38.5 50.4 %collective-permute-start.7 = (bf16[704,2048]{1,0:T(8,128)(2,1)}, bf16[704,2048]{1,0:T(8,128)(2,1)}, u32[]{:S(2)}, u32[]{:S(2)}) collective-permute-start(bf16[704,2048]{1,0:T(8,128)(2,1)} %bitcast.41), channel_id=1, source_target_pairs={{0,2},{2,0},{4,6},{6,4},{8,10},{10,8},{12,14},{14,12},{16,18},{18,... | collective-permute-start | bytes 8650760 | tf_op jit(solution)/shard_map/ppermute | solution.py:16
  38.6 51.3 %collective-permute-start.8 = (bf16[704,2048]{1,0:T(8,128)(2,1)}, bf16[704,2048]{1,0:T(8,128)(2,1)}, u32[]{:S(2)}, u32[]{:S(2)}) collective-permute-start(bf16[704,2048]{1,0:T(8,128)(2,1)} %bitcast.46), channel_id=1, source_target_pairs={{0,2},{2,0},{4,6},{6,4},{8,10},{10,8},{12,14},{14,12},{16,18},{18,... | collective-permute-start | bytes 8650760 | tf_op jit(solution)/shard_map/ppermute | solution.py:16
  39.1 50.8 %collective-permute-start.9 = (bf16[704,2048]{1,0:T(8,128)(2,1)}, bf16[704,2048]{1,0:T(8,128)(2,1)}, u32[]{:S(2)}, u32[]{:S(2)}) collective-permute-start(bf16[704,2048]{1,0:T(8,128)(2,1)} %bitcast.51), channel_id=1, source_target_pairs={{0,2},{2,0},{4,6},{6,4},{8,10},{10,8},{12,14},{14,12},{16,18},{18,... | collective-permute-start | bytes 8650760 | tf_op jit(solution)/shard_map/ppermute | solution.py:16
  87.2 13.8 %collective-permute-start.11 = (bf16[128,1024]{1,0:T(8,128)(2,1)S(1)}, bf16[128,1024]{1,0:T(8,128)(2,1)S(1)}, u32[]{:S(2)}, u32[]{:S(2)}) collective-permute-start(bf16[128,1024]{1,0:T(8,128)(2,1)S(1)} %collective-permute-done.6.refs_0_), channel_id=1, source_target_pairs={{0,4},{2,6},{4,0},{6,2},{8,12},{10,14},{12,8},{14,10},{16,20},{18,... | collective-permute-start | bytes 786440 | tf_op jit(solution)/shard_map/ppermute | solution.py:16
  87.8 13.2 %collective-permute-start.10 = (bf16[128,1024]{1,0:T(8,128)(2,1)S(1)}, bf16[128,1024]{1,0:T(8,128)(2,1)S(1)}, u32[]{:S(2)}, u32[]{:S(2)}) collective-permute-start(bf16[128,1024]{1,0:T(8,128)(2,1)S(1)} %collective-permute-done.6.refs_0_), channel_id=1, source_target_pairs={{0,1},{1,0},{2,3},{3,2},{4,5},{5,4},{6,7},{7,6},{8,9},{9,8},{10,11... | collective-permute-start | bytes 786440 | tf_op jit(solution)/shard_map/ppermute | solution.py:221
  88.9 12.1 %collective-permute-start.12 = (bf16[128,1024]{1,0:T(8,128)(2,1)S(1)}, bf16[128,1024]{1,0:T(8,128)(2,1)S(1)}, u32[]{:S(2)}, u32[]{:S(2)}) collective-permute-start(bf16[128,1024]{1,0:T(8,128)(2,1)S(1)} %add_convert_fusion.4.refs_0_), channel_id=1, source_target_pairs={{0,16},{2,18},{4,20},{6,22},{8,24},{10,26},{12,28},{14,30},{16,0},... | collective-permute-start | bytes 786440 | tf_op jit(solution)/shard_map/ppermute | solution.py:16
  101.1 11.4 %collective-permute-start.15 = (bf16[128,1024]{1,0:T(8,128)(2,1)S(1)}, bf16[128,1024]{1,0:T(8,128)(2,1)S(1)}, u32[]{:S(2)}, u32[]{:S(2)}) collective-permute-start(bf16[128,1024]{1,0:T(8,128)(2,1)S(1)} %collective-permute-done.12.refs_0_), channel_id=1, source_target_pairs={{0,4},{2,6},{4,0},{6,2},{8,12},{10,14},{12,8},{14,10},{16,20},{18,... | collective-permute-start | bytes 786440 | tf_op jit(solution)/shard_map/ppermute | solution.py:16
  102.0 10.5 %collective-permute-start.14 = (bf16[128,1024]{1,0:T(8,128)(2,1)S(1)}, bf16[128,1024]{1,0:T(8,128)(2,1)S(1)}, u32[]{:S(2)}, u32[]{:S(2)}) collective-permute-start(bf16[128,1024]{1,0:T(8,128)(2,1)S(1)} %collective-permute-done.12.refs_0_), channel_id=1, source_target_pairs={{0,1},{1,0},{2,3},{3,2},{4,5},{5,4},{6,7},{7,6},{8,9},{9,8},{10,11... | collective-permute-start | bytes 786440 | tf_op jit(solution)/shard_map/ppermute | solution.py:221
  103.5 8.9 %collective-permute-start.13 = (bf16[128,1024]{1,0:T(8,128)(2,1)S(1)}, bf16[128,1024]{1,0:T(8,128)(2,1)S(1)}, u32[]{:S(2)}, u32[]{:S(2)}) collective-permute-start(bf16[128,1024]{1,0:T(8,128)(2,1)S(1)} %broadcast_select_fusion.2), channel_id=1, source_target_pairs={{0,1},{1,0},{2,6},{3,7},{4,5},{5,4},{6,2},{7,3},{8,9},{9,8},{10,14... | collective-permute-start | bytes 786440 | tf_op jit(solution)/shard_map/ppermute | solution.py:229
  110.9 29.3 %collective-permute-start.21 = (bf16[128,1024]{1,0:T(8,128)(2,1)}, bf16[128,1024]{1,0:T(8,128)(2,1)S(1)}, u32[]{:S(2)}, u32[]{:S(2)}) collective-permute-start(bf16[128,1024]{1,0:T(8,128)(2,1)} %get-tuple-element.123), channel_id=1, source_target_pairs={{0,1},{1,0},{2,6},{3,7},{4,5},{5,4},{6,2},{7,3},{8,9},{9,8},{10,14... | collective-permute-start | bytes 786440 | tf_op jit(solution)/shard_map/ppermute | solution.py:229
  112.5 14.4 %collective-permute-start.18 = (bf16[128,1024]{1,0:T(8,128)(2,1)S(1)}, bf16[128,1024]{1,0:T(8,128)(2,1)S(1)}, u32[]{:S(2)}, u32[]{:S(2)}) collective-permute-start(bf16[128,1024]{1,0:T(8,128)(2,1)S(1)} %collective-permute-done.16.refs_0_), channel_id=1, source_target_pairs={{0,4},{2,6},{4,0},{6,2},{8,12},{10,14},{12,8},{14,10},{16,20},{18,... | collective-permute-start | bytes 786440 | tf_op jit(solution)/shard_map/ppermute | solution.py:16
  113.7 13.2 %collective-permute-start.17 = (bf16[128,1024]{1,0:T(8,128)(2,1)S(1)}, bf16[128,1024]{1,0:T(8,128)(2,1)S(1)}, u32[]{:S(2)}, u32[]{:S(2)}) collective-permute-start(bf16[128,1024]{1,0:T(8,128)(2,1)S(1)} %collective-permute-done.16.refs_0_), channel_id=1, source_target_pairs={{0,1},{1,0},{2,3},{3,2},{4,5},{5,4},{6,7},{7,6},{8,9},{9,8},{10,11... | collective-permute-start | bytes 786440 | tf_op jit(solution)/shard_map/ppermute | solution.py:221
  114.7 12.2 %collective-permute-start.19 = (bf16[128,1024]{1,0:T(8,128)(2,1)S(1)}, bf16[128,1024]{1,0:T(8,128)(2,1)S(1)}, u32[]{:S(2)}, u32[]{:S(2)}) collective-permute-start(bf16[128,1024]{1,0:T(8,128)(2,1)S(1)} %broadcast_select_fusion.1), channel_id=1, source_target_pairs={{0,1},{1,0},{2,6},{3,7},{4,5},{5,4},{6,2},{7,3},{8,9},{9,8},{10,14... | collective-permute-start | bytes 786440 | tf_op jit(solution)/shard_map/ppermute | solution.py:229
  127.1 13.2 %collective-permute-start.20 = (bf16[128,1024]{1,0:T(8,128)(2,1)S(1)}, bf16[128,1024]{1,0:T(8,128)(2,1)S(1)}, u32[]{:S(2)}, u32[]{:S(2)}) collective-permute-start(bf16[128,1024]{1,0:T(8,128)(2,1)S(1)} %broadcast_select_fusion), channel_id=1, source_target_pairs={{0,1},{1,0},{2,6},{3,7},{4,5},{5,4},{6,2},{7,3},{8,9},{9,8},{10,14... | collective-permute-start | bytes 786440 | tf_op jit(solution)/shard_map/ppermute | solution.py:229
  128.0 12.2 %collective-permute-start.22 = (bf16[128,1024]{1,0:T(8,128)(2,1)}, bf16[128,1024]{1,0:T(8,128)(2,1)S(1)}, u32[]{:S(2)}, u32[]{:S(2)}) collective-permute-start(bf16[128,1024]{1,0:T(8,128)(2,1)} %get-tuple-element.124), channel_id=1, source_target_pairs={{0,1},{1,0},{2,6},{3,7},{4,5},{5,4},{6,2},{7,3},{8,9},{9,8},{10,14... | collective-permute-start | bytes 786440 | tf_op jit(solution)/shard_map/ppermute | solution.py:229
  140.3 16.2 %collective-permute-start.26 = (bf16[128,1024]{1,0:T(8,128)(2,1)S(1)}, bf16[128,1024]{1,0:T(8,128)(2,1)S(1)}, u32[]{:S(2)}, u32[]{:S(2)}) collective-permute-start(bf16[128,1024]{1,0:T(8,128)(2,1)S(1)} %get-tuple-element.171), channel_id=1, source_target_pairs={{0,4},{2,6},{4,0},{6,2},{8,12},{10,14},{12,8},{14,10},{16,20},{18,... | collective-permute-start | bytes 786440 | tf_op jit(solution)/shard_map/ppermute | solution.py:16
  141.2 15.3 %collective-permute-start.25 = (bf16[128,1024]{1,0:T(8,128)(2,1)S(1)}, bf16[128,1024]{1,0:T(8,128)(2,1)S(1)}, u32[]{:S(2)}, u32[]{:S(2)}) collective-permute-start(bf16[128,1024]{1,0:T(8,128)(2,1)S(1)} %get-tuple-element.172), channel_id=1, source_target_pairs={{0,1},{1,0},{2,3},{3,2},{4,5},{5,4},{6,7},{7,6},{8,9},{9,8},{10,11... | collective-permute-start | bytes 786440 | tf_op jit(solution)/shard_map/ppermute | solution.py:221
  142.8 13.7 %collective-permute-start.24 = (bf16[128,1024]{1,0:T(8,128)(2,1)S(1)}, bf16[128,1024]{1,0:T(8,128)(2,1)S(1)}, u32[]{:S(2)}, u32[]{:S(2)}) collective-permute-start(bf16[128,1024]{1,0:T(8,128)(2,1)S(1)} %get-tuple-element.173), channel_id=1, source_target_pairs={{0,4},{2,6},{4,0},{6,2},{8,12},{10,14},{12,8},{14,10},{16,20},{18,... | collective-permute-start | bytes 786440 | tf_op jit(solution)/shard_map/ppermute | solution.py:16
  143.4 13.1 %collective-permute-start.23 = (bf16[128,1024]{1,0:T(8,128)(2,1)S(1)}, bf16[128,1024]{1,0:T(8,128)(2,1)S(1)}, u32[]{:S(2)}, u32[]{:S(2)}) collective-permute-start(bf16[128,1024]{1,0:T(8,128)(2,1)S(1)} %get-tuple-element.174), channel_id=1, source_target_pairs={{0,1},{1,0},{2,3},{3,2},{4,5},{5,4},{6,7},{7,6},{8,9},{9,8},{10,11... | collective-permute-start | bytes 786440 | tf_op jit(solution)/shard_map/ppermute | solution.py:221
  144.6 12.0 %collective-permute-start.27 = (bf16[128,1024]{1,0:T(8,128)(2,1)}, bf16[128,1024]{1,0:T(8,128)(2,1)S(1)}, u32[]{:S(2)}, u32[]{:S(2)}) collective-permute-start(bf16[128,1024]{1,0:T(8,128)(2,1)} %get-tuple-element.136), channel_id=1, source_target_pairs={{0,1},{1,0},{2,6},{3,7},{4,5},{5,4},{6,2},{7,3},{8,9},{9,8},{10,14... | collective-permute-start | bytes 786440 | tf_op jit(solution)/shard_map/ppermute | solution.py:229
  158.7 9.8 %collective-permute-start.30 = (bf16[128,1024]{1,0:T(8,128)(2,1)}, bf16[128,1024]{1,0:T(8,128)(2,1)S(1)}, u32[]{:S(2)}, u32[]{:S(2)}) collective-permute-start(bf16[128,1024]{1,0:T(8,128)(2,1)} %get-tuple-element.142), channel_id=1, source_target_pairs={{0,1},{1,0},{2,6},{3,7},{4,5},{5,4},{6,2},{7,3},{8,9},{9,8},{10,14... | collective-permute-start | bytes 786440 | tf_op jit(solution)/shard_map/ppermute | solution.py:229
  160.4 9.5 %collective-permute-start.31 = (bf16[128,1024]{1,0:T(8,128)(2,1)S(1)}, bf16[128,1024]{1,0:T(8,128)(2,1)S(1)}, u32[]{:S(2)}, u32[]{:S(2)}) collective-permute-start(bf16[128,1024]{1,0:T(8,128)(2,1)S(1)} %add_convert_fusion.3), channel_id=1, source_target_pairs={{0,8},{2,10},{4,12},{6,14},{8,16},{10,18},{12,20},{14,22},{16,24},... | collective-permute-start | bytes 786440 | tf_op jit(solution)/shard_map/ppermute | solution.py:16
  172.5 12.0 %collective-permute-start.34 = (bf16[128,1024]{1,0:T(8,128)(2,1)S(1)}, bf16[128,1024]{1,0:T(8,128)(2,1)S(1)}, u32[]{:S(2)}, u32[]{:S(2)}) collective-permute-start(bf16[128,1024]{1,0:T(8,128)(2,1)S(1)} %add_convert_fusion.2), channel_id=1, source_target_pairs={{0,16},{2,18},{4,20},{6,22},{8,24},{10,26},{12,28},{14,30},{16,0},... | collective-permute-start | bytes 786440 | tf_op jit(solution)/shard_map/ppermute | solution.py:16
  (52 other events, 678.5 us)
